TPU v7x, 32 devices: a whole 2x2x4 slice. The times are simulated.
32 devices in a mesh: narrow: 4 (over y, x), wide: 8 (over z, core).
Axes of the slice: x: 2, y: 2, z: 4, core: 2. Of those that a mesh axis runs over, the one named last changes fastest.
Arguments:
- tokens: float32 [2048, 768], P('wide'), may hold values from -6 to 6
- norm1_gain: float32 [768], replicated, may hold values from 0.5 to 1.5
- in_weight: float32 [768, 2, 1536], P(None, None, 'narrow'), may hold values from -0.21875 to 0.21875
- conv_weight: float32 [4, 1536], P(None, 'narrow'), may hold values from -3 to 3
- conv_bias: float32 [1536], P('narrow'), may hold values from -1.5 to 1.5
- xproj_weight: float32 [1536, 80], P('narrow'), may hold values from -0.15625 to 0.15625
- dt_weight: float32 [48, 1536], P(None, 'narrow'), may hold values from -0.875 to 0.875
- dt_bias: float32 [1536], P('narrow'), may hold values from -6 to -2
- decay_log: float32 [16, 1536], P(None, 'narrow'), may hold values from -6 to 2.5
- skip_gain: float32 [1536], P('narrow'), may hold values from 0.5 to 1.5
- out_weight: float32 [1536, 768], P('narrow'), may hold values from -0.15625 to 0.15625
- norm2_gain: float32 [768], replicated, may hold values from 0.5 to 1.5
- router_weight: float32 [768, 8], replicated, may hold values from -0.15625 to 0.15625
- expert_in: float32 [8, 768, 3072], P('wide', None, 'narrow'), may hold values from -0.21875 to 0.21875
- expert_out: float32 [8, 3072, 768], P('wide', 'narrow'), may hold values from -1.5 to 1.5
- segments: int32 [2048], replicated, may hold values from -1 to 24, as said below
- expert_ids: int32 [2048, 1], P('wide'), may hold values from 0 to 7; in each aligned block of 256 rows (0 to 255, 256 to 511, ...) at most 51 rows name the same one
- cotangent: float32 [2048, 768], P('wide'), may hold values from -6 to 6
Outputs:
- output: float32 [2048, 768], P('wide')
- grad_tokens: float32 [2048, 768], P('wide')
- grad_norm1_gain: float32 [768], replicated
- grad_in_weight: float32 [768, 2, 1536], P(None, None, 'narrow')
- grad_conv_weight: float32 [4, 1536], P(None, 'narrow')
- grad_conv_bias: float32 [1536], P('narrow')
- grad_xproj_weight: float32 [1536, 80], P('narrow')
- grad_dt_weight: float32 [48, 1536], P(None, 'narrow')
- grad_dt_bias: float32 [1536], P('narrow')
- grad_decay_log: float32 [16, 1536], P(None, 'narrow')
- grad_skip_gain: float32 [1536], P('narrow')
- grad_out_weight: float32 [1536, 768], P('narrow')
- grad_norm2_gain: float32 [768], replicated
- grad_router_weight: float32 [768, 8], replicated
- grad_expert_in: float32 [8, 768, 3072], P('wide', None, 'narrow')
- grad_expert_out: float32 [8, 3072, 768], P('wide', 'narrow')
Inputs may be any that keep to these rules, and one draw needn't show every extreme that they name: `segments`: document numbers never fall; each document's number is one more than the previous document's; -1 marks padding, which forms one run at the end of the stream, after the last document, whose number is the largest. Apart from the first, which begins at token 0, every document and the padding begin at least 32 tokens away from either edge of an aligned block of 256 tokens; every document is shorter than 1024 tokens. `expert_ids`: in each aligned block of 256 rows no expert is named by more than 51 rows.
All inputs are finite; a program needn't handle non-finite values.
Results may differ from a plain program's by a relative error of at most 0.0003.
Values sent between devices are 32-bit elements; how exact they have to be, the bound alone decides.
No kernel may reach another device: no remote copies, remote signals or barrier semaphores. Data moves between devices by JAX's collectives and lax.ppermute only.
A program may use at most 192 MiB of HBM per device.

v0:
```python
import functools
import math

import jax
import jax.numpy as jnp
from jax import lax
from jax.experimental import pallas as pl
from jax.experimental.pallas import tpu as pltpu
from jax.sharding import PartitionSpec as P

EPSILON = 1e-05
SEGMENTS = 8
LANES = 128
NEVER = 1e30
VMEM_SPARE = 4 * 1024 * 1024
GROUP = 4
LOG2E = 1.4426950408889634


def shape_of(*shape, dtype=jnp.float32):
    return jax.ShapeDtypeStruct(shape, dtype)


def call(kernel, outs, ids, *arrays, scratch=(), after=(), far_in=(), out_place=(), in_place=()):
    in_vmem = pl.BlockSpec(memory_space=pltpu.VMEM)
    anywhere = pl.BlockSpec(memory_space=pl.ANY)
    far = pl.BlockSpec(memory_space=pltpu.HBM)
    arrays = [
        pltpu.with_memory_space_constraint(array, pltpu.HBM) if i in far_in else array
        for i, array in enumerate(arrays)
    ]
    size = lambda a: math.prod(a.shape) * jnp.dtype(a.dtype).itemsize
    held = [
        size(a)
        for refs, skipped in ((arrays, (*in_place, *far_in)), (outs, out_place))
        for i, a in enumerate(refs)
        if i not in skipped
    ]
    held += [size(a) for a in scratch if hasattr(a, "dtype") and hasattr(a, "shape")
             and jnp.issubdtype(a.dtype, jnp.number)]
    given = 1 + len(arrays)

    def run(*refs):
        kernel(*refs[:given], *refs[given + len(after) :])

    return pl.pallas_call(
        run,
        out_shape=outs,
        in_specs=[pl.BlockSpec(memory_space=pltpu.SMEM)]
        + [far if i in far_in else anywhere if i in in_place else in_vmem
           for i in range(len(arrays))]
        + [anywhere] * len(after),
        out_specs=[anywhere if i in out_place else in_vmem for i in range(len(outs))],
        scratch_shapes=scratch,
        compiler_params=pltpu.CompilerParams(vmem_limit_bytes=sum(held) + VMEM_SPARE),
        cost_estimate=pl.CostEstimate(flops=1, bytes_accessed=1, transcendentals=0),
    )(ids, *arrays, *after)


def two_parts(value):
    high = value.astype(jnp.bfloat16)
    return high, (value - high.astype(jnp.float32)).astype(jnp.bfloat16)


def once(left, right, contract=(1, 0)):
    return lax.dot_general(
        left,
        right,
        (((contract[0],), (contract[1],)), ((), ())),
        preferred_element_type=jnp.float32,
    )


def product(left, right, contract=(1, 0)):
    left_high, left_low = left if isinstance(left, tuple) else two_parts(left)
    right_high, right_low = right if isinstance(right, tuple) else two_parts(right)
    free = 1 - contract[0]
    size = left_high.shape[free]
    if size % (16, LANES)[free]:
        return once(left_high, right_high, contract) + (
            once(left_high, right_low, contract) + once(left_low, right_high, contract)
        )
    both = once(jnp.concatenate([left_high, left_low], axis=free), right_high, contract)
    return both[:size] + (both[size:] + once(left_high, right_low, contract))


def select_rows(chosen, rows, contract=(1, 0)):
    high, low = two_parts(rows)
    return once(chosen, high, contract) + once(chosen, low, contract)


def inverse_rms(rows):
    return lax.rsqrt(jnp.mean(rows * rows, axis=-1, keepdims=True) + EPSILON)


def norm_back(rows, inverse, gain, grad):
    scaled = gain * grad
    mean = jnp.mean(rows * scaled, axis=-1, keepdims=True)
    return inverse * scaled - rows * (inverse * inverse * inverse) * mean


def sigmoid(value):
    return 1.0 / (1.0 + jnp.exp(-value))


def softplus(value):
    return jnp.maximum(value, 0.0) + jnp.log1p(jnp.exp(-jnp.abs(value)))


def gelu_parts(value):
    spread_of = 0.5 * (1.0 + lax.erf(value * (0.5**0.5)))
    density = jnp.exp(-0.5 * value * value) * ((2.0 * jnp.pi) ** -0.5)
    return value * spread_of, spread_of + value * density


def cut_slices(me, whole, out):
    rows, part = whole.shape[0] // 2, whole.shape[1] // 4
    for j in range(4):
        out[me ^ j, :, :part] = whole[:rows, part * j : part * (j + 1)]
        out[me ^ j, :, part:] = whole[rows:, part * j : part * (j + 1)]


def join_slices(me, parts, held, whole):
    rows, part = whole.shape[0] // 2, whole.shape[1] // 4
    for key, value in enumerate(parts):
        held[key] = value[...]
    for j in range(4):
        value = held[me ^ j]
        whole[:rows, part * j : part * (j + 1)] = value[:, :part]
        whole[rows:, part * j : part * (j + 1)] = value[:, part:]


def reversed_bits(value, levels):
    place = 0
    for level in range(levels):
        place = place + (((value >> level) & 1) << (levels - 1 - level))
    return place


def interleave_from(rows, held, out):
    length, width = out.shape
    steps = length // SEGMENTS
    for tile in range(width // LANES):
        lanes = slice(tile * LANES, (tile + 1) * LANES)
        held[tile] = rows[:, lanes]
        for step in range(steps):
            out[step * SEGMENTS : (step + 1) * SEGMENTS, lanes] = held[
                tile, pl.ds(step, SEGMENTS, stride=steps), :
            ]


def deinterleave_to(rows, held, out):
    length, width = out.shape
    steps = length // SEGMENTS
    for tile in range(width // LANES):
        lanes = slice(tile * LANES, (tile + 1) * LANES)
        for step in range(steps):
            held[tile, pl.ds(step, SEGMENTS, stride=steps), :] = rows[
                step * SEGMENTS : (step + 1) * SEGMENTS, lanes
            ]
        out[:, lanes] = held[tile]


def narrow_swap(value, key):
    return lax.ppermute(value, "narrow", [(i, i ^ key) for i in range(4)])


def core_swap(value):
    count = lax.axis_size("wide")
    return lax.ppermute(value, "wide", [(i, i ^ 1) for i in range(count)])


def chip_swap(value, key):
    count = lax.axis_size("wide")
    return lax.ppermute(value, "wide", [(i, i ^ (2 * key)) for i in range(count)])


def wide_shift(value, distance):
    devices = range(lax.axis_size("wide"))
    route = [(i - distance, i) for i in devices if i - distance in devices]
    return lax.ppermute(value, "wide", route)


def hold(value, *others):
    if not others:
        return value
    return lax.optimization_barrier((value, others))[0]


def narrow_all(value):
    far = narrow_swap(value, 3)
    return [value, narrow_swap(value, 1), narrow_swap(value, 2), far]


def narrow_each(slices):
    far = narrow_swap(slices[3], 3)
    return [slices[0], narrow_swap(slices[1], 1), narrow_swap(slices[2], 2), far]


def pair_sum(parts):
    while len(parts) > 1:
        parts = [a + b for a, b in zip(parts[::2], parts[1::2])]
    return parts[0]


def chip_blocks(blocks, chips):
    rows = blocks.shape[0] // chips
    order = sorted(range(1, chips), reverse=True)
    arrived = {k: chip_swap(blocks[k * rows : (k + 1) * rows], k) for k in order}
    arrived[0] = blocks[:rows]
    return [arrived[k] for k in range(chips)]


def chip_each(blocks, chips):
    return jnp.concatenate(chip_blocks(blocks, chips))


def chip_all(value, chips):
    arrived = {k: chip_swap(value, k) for k in sorted(range(1, chips), reverse=True)}
    arrived[0] = value
    return [arrived[k] for k in range(chips)]


class WideSum:
    def __init__(self, keep, send):
        levels = lax.axis_size("wide").bit_length() - 1
        self.swaps = [core_swap] + [
            functools.partial(chip_swap, key=1 << level) for level in range(levels - 1)
        ]
        self.keep, self.send, self.arrived = keep, send, None
        self.level, self.back = 0, False

    def prepare(self):
        if not self.back and self.level == len(self.swaps):
            self.back = True
        if self.back:
            self.level -= 1
            self.send = self.keep
        return self.send

    def start(self, *others):
        self.prepare()
        self.arrived = self.swaps[self.level](hold(self.send, *others))
        return self.arrived

    def start_with(self, rider):
        sent = self.prepare()
        joined = jnp.concatenate([sent.reshape(1, -1, sent.shape[2]), rider], axis=1)
        arrived = self.swaps[self.level](joined)
        rows = rider.shape[1]
        self.arrived = arrived[:, :-rows].reshape(sent.shape)
        return self.arrived, arrived[:, -rows:]

    def finish(self, *others):
        arrived = hold(self.arrived, *others) if others else self.arrived
        if self.back:
            self.keep = jnp.concatenate([self.keep, arrived])
            return
        self.level += 1
        if self.level == len(self.swaps):
            self.keep = self.keep + arrived
            return
        half = self.keep.shape[0] // 2
        self.send = self.keep[half:] + arrived[half:]
        self.keep = self.keep[:half] + arrived[:half]

    def rest(self):
        while not (self.back and self.level == 0):
            self.start()
            self.finish()
        return self.keep


def start_both(one, two, *others):
    first, second = one.prepare(), two.prepare()
    rows = first.shape[1]
    arrived = one.swaps[one.level](hold(jnp.concatenate([first, second], axis=1), *others))
    one.arrived, two.arrived = arrived[:, :rows], arrived[:, rows:]
    return one.arrived, two.arrived


def route_kernel(capacity, ids, segments, expert_ids, marks, slots_own, slots_other,
                 rows_own, rows_other):
    wide_at, core, chip = ids[1], ids[2], ids[3]
    length = expert_ids.shape[1]
    per = length // LANES
    experts = segments.shape[0] // per
    steps = length // SEGMENTS

    def block(at):
        return jnp.concatenate([segments[pl.ds(at * per + i, 1), :] for i in range(per)], axis=1)

    own, before = block(wide_at), block(jnp.maximum(wide_at - 1, 0))
    lane = lax.broadcasted_iota(jnp.int32, (1, length), 1)
    here = lax.broadcasted_iota(jnp.int32, (SEGMENTS, length), 0)
    table = jnp.ones((SEGMENTS, length), jnp.float32)
    for k in range(1, 4):
        back = jnp.where(lane < k, pltpu.roll(before, k, 1), pltpu.roll(own, k, 1))
        same = (back == own) & ((lane >= k) | (wide_at > 0))
        table = jnp.where(here == k, jnp.where(same, 1.0, 0.0), table)
    live = own >= 0
    expert = expert_ids[...]
    at = lax.broadcasted_iota(jnp.int32, (experts, length), 0)
    hits = jnp.where((at == expert) & live, 1.0, 0.0)
    first = lax.broadcasted_iota(jnp.int32, (length, length), 0)
    second = lax.broadcasted_iota(jnp.int32, (length, length), 1)
    earlier = jnp.where(first < second, 1.0, 0.0).astype(jnp.bfloat16)
    ranks = once(hits.astype(jnp.bfloat16), earlier)
    rank = jnp.sum(ranks * hits, axis=0, keepdims=True).astype(jnp.int32)
    kept = live & (rank < capacity)
    order = jnp.where(
        (first % SEGMENTS) * steps + first // SEGMENTS == second, 1.0, 0.0
    ).astype(jnp.bfloat16)
    marks[...] = once(order, table.astype(jnp.bfloat16), (1, 1))
    slot = jnp.where(kept, ((expert >> 1) ^ chip) * capacity + rank, -1)
    count = slots_own.shape[0]
    slot_at = lax.broadcasted_iota(jnp.int32, (count, length), 0)
    for which, slots, rows in ((core, slots_own, rows_own), (1 - core, slots_other, rows_other)):
        mine = (slot_at == slot) & ((expert & 1) == which)
        chosen = jnp.where(mine, 1.0, 0.0).astype(jnp.bfloat16)
        slots[...] = once(chosen, order, (1, 1)).astype(jnp.bfloat16)
        rows[...] = once(order, chosen, (1, 1)).astype(jnp.bfloat16)


def front_kernel(ids, tokens, gain, conv_high, conv_low, gate_high, gate_low,
                 rows, normed, conv_in, gate_in, held):
    interleave_from(tokens, held, rows)
    value = rows[...]
    scaled = value * inverse_rms(value) * gain[...][None]
    normed[...] = scaled
    parts = two_parts(scaled)
    conv_in[...] = product(parts, (conv_high[...], conv_low[...]))
    gate_in[...] = product(parts, (gate_high[...], gate_low[...]))


def start_kernel(capacity, ids, segments_far, expert_ids_far, tokens_far, cotangent_far, weight_far,
                 marks, slots_own, slots_other, rows_own, rows_other,
                 rows_slice, cot_slice, own, other, conv_high, conv_low, gate_high, gate_low,
                 segments, expert_ids, tokens, cotangent, weight, rows, held, branch,
                 sems):
    pairs = (
        (segments_far, segments),
        (expert_ids_far, expert_ids),
        (tokens_far, tokens),
        (cotangent_far, cotangent),
        (weight_far, weight),
    )
    copies = [
        pltpu.make_async_copy(far, near, sems.at[i]) for i, (far, near) in enumerate(pairs)
    ]
    for copy in copies:
        copy.start()
    copies[0].wait()
    copies[1].wait()
    route_kernel(capacity, ids, segments, expert_ids, marks, slots_own, slots_other,
                 rows_own, rows_other)
    copies[2].wait()
    copies[3].wait()
    slices_kernel(ids, tokens, cotangent, slots_own, slots_other, rows_slice, cot_slice, own, other,
                  rows, held)
    copies[4].wait()
    for k, (high, low) in enumerate(((conv_high, conv_low), (gate_high, gate_low))):
        branch[k] = weight[:, k, :]
        high[...], low[...] = two_parts(branch[k])


def slices_kernel(ids, tokens, cotangent, slots_own, slots_other,
                  rows_slice, cot_slice, own, other, rows, held):
    me, core = ids[0], ids[2]
    half, part = tokens.shape[0] // 2, tokens.shape[1] // 4
    for source, out in ((tokens, rows_slice), (cotangent, cot_slice)):
        interleave_from(source, held, rows)
        for j in range(4):
            @pl.when(me == j)
            def _():
                out[:, :part] = rows[:half, part * j : part * (j + 1)]
                out[:, part:] = rows[half:, part * j : part * (j + 1)]
    send_slots(core, cot_slice[...], slots_own[...], slots_other[...], own, other)


def send_slots(core, packed, slots_own, slots_other, own, other):
    half = packed.shape[1] // 2
    lane = lax.broadcasted_iota(jnp.int32, packed.shape, 1)
    left = jnp.where(lane < half, packed, 0.0)
    right = jnp.where(lane < half, 0.0, packed)
    second = core == 1
    top = jnp.where(second, pltpu.roll(left, half, 1), left)
    bottom = jnp.where(second, right, pltpu.roll(right, half, 1))
    placed = jnp.concatenate([top, bottom])
    own[...] = select_rows(slots_own, placed)
    other[...] = select_rows(slots_other, placed)


def conv_kernel(ids, halo, gain, conv_high, conv_low, conv_in, marks, conv_weight, conv_bias,
                xproj_t, mixed, conv_out, partial, extended, halo_normed):
    taps, channels = conv_weight.shape
    length = conv_in.shape[0]
    lead = (taps - 1) * SEGMENTS
    rows = halo[...]
    scaled = rows * inverse_rms(rows) * gain[...][None]
    halo_normed[...] = scaled
    halo_conv = product(scaled, (conv_high[...], conv_low[...]))
    place = lax.broadcasted_iota(jnp.int32, (SEGMENTS, channels), 0)
    for m in range(taps - 1):
        ends = conv_in[length - lead + m * SEGMENTS : length - lead + (m + 1) * SEGMENTS, :]
        at = SEGMENTS - taps + 1 + m
        extended[m * SEGMENTS : (m + 1) * SEGMENTS, :] = jnp.where(
            place == 0, halo_conv[at : at + 1, :], pltpu.roll(ends, 1, 0)
        )
    extended[lead:, :] = conv_in[...]
    total = jnp.broadcast_to(conv_bias[...][None], (length, channels))
    for k in range(taps):
        first = (taps - 1 - k) * SEGMENTS
        total += conv_weight[k : k + 1, :] * extended[first : first + length, :] * marks[:, k : k + 1]
    mixed[...] = total
    out = total * sigmoid(total)
    conv_out[...] = out
    partial[...] = product(xproj_t[...], out, (1, 1))


def rows_at(step):
    return pl.ds(pl.multiple_of(step * SEGMENTS, SEGMENTS), SEGMENTS)


def spread(row):
    return jnp.broadcast_to(row, (SEGMENTS, row.shape[-1]))


def column_of(rows, column):
    return jnp.broadcast_to(rows[:, column : column + 1], (SEGMENTS, LANES))


def sweep(count, body, carry):
    return lax.fori_loop(0, count, body, carry, unroll=True)


def add_to(ref, first, rows, lanes, value):
    if first:
        ref[rows, lanes] = value
    else:
        ref[rows, lanes] += value


def chain_pieces(decay, value, backward):
    place = lax.broadcasted_iota(jnp.int32, decay.shape, 0)
    if backward:
        place = SEGMENTS - 1 - place

    def moved(array, distance):
        return pltpu.roll(array, (SEGMENTS - distance) if backward else distance, 0)

    distance = 1
    while distance < SEGMENTS:
        inside = place >= distance
        value = jnp.where(inside, decay * moved(value, distance) + value, value)
        decay = jnp.where(inside, decay * moved(decay, distance), decay)
        distance *= 2
    first = place == 0
    before = jnp.where(first, 0.0, moved(value, 1))
    factor = jnp.where(first, 1.0, moved(decay, 1))
    return factor, before, value


def totals_kernel(ids, p0, p1, p2, p3, dt_weight, dt_bias, decay_log, conv_out, marks,
                  coef, dt_pre, stepsize, drive, stepd, rates, entry, total, padded):
    states, channels = decay_log.shape
    rank = dt_weight.shape[0]
    length = conv_out.shape[0]
    steps = length // SEGMENTS
    projected = (p0[...] + p1[...]) + (p2[...] + p3[...])
    missing = LANES - projected.shape[0]
    coef[...] = jnp.concatenate([projected, jnp.zeros((missing, length), jnp.float32)]).T
    padded[...] = jnp.zeros_like(padded)
    padded[:rank, :] = dt_weight[...]
    pre = product(coef[...], padded[...]) + dt_bias[...][None]
    dt_pre[...] = pre
    size = softplus(pre)
    stepsize[...] = size
    drive[...] = size * conv_out[...]
    stepd[...] = jnp.where(marks[:, 1:2] > 0.5, size, NEVER)
    rates[...] = -jnp.exp(decay_log[...])
    total[...] = jnp.zeros_like(total)
    zero = jnp.zeros((SEGMENTS, LANES), jnp.float32)
    tiles = [slice(at, at + LANES) for at in range(0, channels, LANES)]
    sums = [zero] * len(tiles)
    for step in range(steps):
        rows = slice(step * SEGMENTS, (step + 1) * SEGMENTS)
        sums = [value + stepd[rows, lanes] for value, lanes in zip(sums, tiles)]
    for value, lanes in zip(sums, tiles):
        total[states : states + 1, lanes] = jnp.sum(value, axis=0, keepdims=True)
    for group in range(0, states, GROUP):
        names = range(group, group + GROUP)
        rate = [[spread(rates[n : n + 1, lanes] * LOG2E) for lanes in tiles] for n in names]

        def body(step, current):
            rows = rows_at(step)
            near = coef[rows, :]
            width = [stepd[rows, lanes] for lanes in tiles]
            push = [drive[rows, lanes] for lanes in tiles]
            later = []
            for at, n in enumerate(names):
                entering = column_of(near, rank + n)
                later.append(tuple(
                    jnp.exp2(width[t] * rate[at][t]) * current[at][t] + push[t] * entering
                    for t in range(len(tiles))
                ))
            return tuple(later)

        current = sweep(steps, body, ((zero,) * len(tiles),) * GROUP)
        for at, n in enumerate(names):
            for t, lanes in enumerate(tiles):
                decay = jnp.exp2(sums[t] * rate[at][t])
                factor, before, last = chain_pieces(decay, current[at][t], False)
                entry[0, n, :, lanes] = factor
                entry[1, n, :, lanes] = before
                total[n : n + 1, lanes] = last[SEGMENTS - 1 :, :]


def pair_kernel(ids, total, other, rates, early, late, chip):
    states = rates.shape[0]
    second = ids[2] == 1
    mine, theirs = total[...], other[...]
    first, last = jnp.where(second, theirs, mine), jnp.where(second, mine, theirs)
    early[...] = first
    late[...] = last
    chip[...] = first + last
    chip[:states, :] = (
        jnp.exp(last[states : states + 1] * rates[...]) * first[:states] + last[:states]
    )


def pair_back_kernel(ids, total, other, early, rates, late_total, chip):
    states = rates.shape[0]
    second = ids[2] == 1
    mine, theirs = total[...], other[...]
    first, last = jnp.where(second, theirs, mine), jnp.where(second, mine, theirs)
    late_total[...] = last
    chip[...] = first + jnp.exp(early[states : states + 1, :] * rates[...]) * last


def states_kernel(rank, ids, stepd, drive, coef, rates, entry, early, conv_out, gate_in, skip,
                  out_weight, *rest):
    chips = len(rest) - 8
    totals = rest[:chips]
    ssm_skip, gated, slices, kept, held, whole, kept_here, sems = rest[chips:]
    me, core, here = ids[0], ids[2], ids[3]
    states, channels = rates.shape
    length = stepd.shape[0]
    steps = length // SEGMENTS
    for key, value in enumerate(totals):
        held[key] = value[...]
    state = jnp.zeros((states, channels), jnp.float32)
    for chip in range(chips):
        value = held[here ^ chip]
        grown = jnp.exp(value[states : states + 1] * rates[...]) * state + value[:states]
        state = jnp.where(chip < here, grown, state)
    inner = jnp.exp(early[states : states + 1, :] * rates[...]) * state + early[:states, :]
    start = jnp.where(core == 1, inner, state)
    tiles = [slice(at, at + LANES) for at in range(0, channels, LANES)]
    copies = []
    for group in range(0, states, GROUP):
        names = range(group, group + GROUP)
        slab = group // GROUP
        rate = [[spread(rates[n : n + 1, lanes] * LOG2E) for lanes in tiles] for n in names]
        current = tuple(
            tuple(
                entry[0, n, :, lanes] * start[n : n + 1, lanes] + entry[1, n, :, lanes]
                for lanes in tiles
            )
            for n in names
        )
        for at in range(GROUP):
            for t, lanes in enumerate(tiles):
                kept_here[slab, 0, at, :, lanes] = current[at][t]

        def body(step, current):
            rows = rows_at(step)
            near = coef[rows, :]
            width = [stepd[rows, lanes] for lanes in tiles]
            push = [drive[rows, lanes] for lanes in tiles]
            later, total = [], [None] * len(tiles)
            for at, n in enumerate(names):
                entering, leaving = column_of(near, rank + n), column_of(near, rank + states + n)
                new = []
                for t, lanes in enumerate(tiles):
                    decay = jnp.exp2(width[t] * rate[at][t])
                    new.append(decay * current[at][t] + push[t] * entering)
                    kept_here[slab, step + 1, at, :, lanes] = new[t]
                    term = leaving * new[t]
                    total[t] = term if total[t] is None else total[t] + term
                later.append(tuple(new))
            for t, lanes in enumerate(tiles):
                add_to(ssm_skip, group == 0, rows, lanes, total[t])
            return tuple(later)

        sweep(steps, body, current)
        copies.append(pltpu.make_async_copy(kept_here.at[slab], kept.at[slab], sems.at[slab]))
        copies[-1].start()
    skipped = ssm_skip[...] + skip[...][None] * conv_out[...]
    ssm_skip[...] = skipped
    gate = gate_in[...]
    out = skipped * gate * sigmoid(gate)
    gated[...] = out
    whole[...] = product(out, out_weight[...])
    cut_slices(me, whole, slices)
    for copy in copies:
        copy.wait()


def dispatch_kernel(ids, s0, s1, s2, s3, rows_slice, slots_own, slots_other,
                    hidden, own, other):
    packed = (s0[...] + s1[...]) + (s2[...] + s3[...]) + rows_slice[...]
    hidden[...] = packed
    send_slots(ids[2], packed, slots_own[...], slots_other[...], own, other)


def raw_kernel(ids, c0, c1, c2, c3, expert_in, expert_out, raw, cot, in_high, in_low,
               out_high, out_low, held):
    join_slices(ids[0], (c0, c1, c2, c3), held, cot)
    in_high[...], in_low[...] = two_parts(expert_in[...])
    out_high[...], out_low[...] = two_parts(expert_out[...])
    raw[...] = product(cot[...], (out_high[...], out_low[...]), (1, 1))


def expert_kernel(ids, parts, raw, in_high, in_low, norm_gain, router_t,
                  slices, second, act, grad_pre, gates, grad_logits, grad_gain,
                  whole):
    me, expert = ids[0], ids[1]
    count, part = whole.shape[0] // 2, whole.shape[1] // 4
    for j in range(4):
        whole[:count, part * j : part * (j + 1)] = parts[j, :, :part]
        whole[count:, part * j : part * (j + 1)] = parts[j, :, part:]
    rows = whole[...]
    inverse = inverse_rms(rows)
    normed = rows * inverse * norm_gain[...][None]
    second[...] = normed
    normed_parts = two_parts(normed)
    router_parts = two_parts(router_t[...])
    weight = (in_high[...], in_low[...])
    logits = product(normed_parts, router_parts, (1, 1))
    logits = logits - jnp.max(logits, axis=-1, keepdims=True)
    powers = jnp.exp(logits)
    probs = powers / jnp.sum(powers, axis=-1, keepdims=True)
    chosen = jnp.where(
        lax.broadcasted_iota(jnp.int32, logits.shape, 1) == expert, 1.0, 0.0
    )
    gate = jnp.sum(probs * chosen, axis=-1, keepdims=True)
    gates[...] = gate
    hidden_act, slope = gelu_parts(product(normed_parts, weight))
    act[...] = hidden_act
    raws = raw[...]
    grad_gate = jnp.sum(hidden_act * raws, axis=-1, keepdims=True)
    grads = gate * raws * slope
    grad_pre[...] = grads
    logit_grads = grad_gate * gate * (chosen - probs)
    grad_logits[...] = logit_grads
    grad_second = product(grads, weight, (1, 1)) + product(logit_grads, router_parts)
    grad_gain[...] = jnp.sum(rows * inverse * grad_second, axis=0, keepdims=True)
    whole[...] = norm_back(rows, inverse, norm_gain[...][None], grad_second)
    cut_slices(me, whole, slices)


def expert_rest_kernel(ids, second, act, grad_pre, gates, grad_logits, cot, out_high, out_low,
                       slices, grad_in, grad_out, grad_router, whole):
    gate = gates[...]
    acts = two_parts(act[...])
    normed = two_parts(second[...])
    whole[...] = gate * product(acts, (out_high[...], out_low[...]))
    cut_slices(ids[0], whole, slices)
    grad_out[...] = product(acts, gate * cot[...], (0, 0))
    grad_in[...] = product(normed, grad_pre[...], (0, 0))
    grad_router[...] = product(grad_logits[...], normed, (0, 0))


def home_kernel(ids, own, other, base, rows_own, rows_other, out):
    half = own.shape[1] // 2
    second = ids[2] == 1

    def mine(rows):
        return jnp.where(second, pltpu.roll(rows, half, 1), rows)

    total = select_rows(rows_own[...], mine(own[...])) + select_rows(
        rows_other[...], mine(other[...])
    )
    count = base.shape[0]
    lane = lax.broadcasted_iota(jnp.int32, base.shape, 1)
    out[...] = base[...] + jnp.where(
        lane < half, total[:count], pltpu.roll(total[count:], half, 1)
    )


def whole_kernel(ids, p0, p1, p2, p3, out, held, whole, tiles):
    join_slices(ids[0], (p0, p1, p2, p3), held, whole)
    deinterleave_to(whole, tiles, out)


def leaving_kernel(rank, ids, g0, g1, g2, g3, out_weight, gate_in, ssm_skip, conv_out, stepd,
                   coef, rates, grad_hidden, grad_ssm, grad_gate_in, grad_skip, entry, total,
                   held):
    join_slices(ids[0], (g0, g1, g2, g3), held, grad_hidden)
    states, channels = rates.shape
    length = stepd.shape[0]
    steps = length // SEGMENTS
    grad_gated = product(grad_hidden[...], out_weight[...], (1, 1))
    gate = gate_in[...]
    gate_sigmoid = sigmoid(gate)
    pulled = grad_gated * gate * gate_sigmoid
    grad_ssm[...] = pulled
    grad_gate_in[...] = grad_gated * ssm_skip[...] * (
        gate_sigmoid * (1.0 + gate * (1.0 - gate_sigmoid))
    )
    grad_skip[...] = jnp.sum(pulled * conv_out[...], axis=0, keepdims=True)
    zero = jnp.zeros((SEGMENTS, LANES), jnp.float32)
    tiles = [slice(at, at + LANES) for at in range(0, channels, LANES)]
    sums = [zero] * len(tiles)
    for step in range(steps):
        rows = slice(step * SEGMENTS, (step + 1) * SEGMENTS)
        sums = [value + stepd[rows, lanes] for value, lanes in zip(sums, tiles)]
    for group in range(0, states, GROUP):
        names = range(group, group + GROUP)
        rate = [[spread(rates[n : n + 1, lanes] * LOG2E) for lanes in tiles] for n in names]

        def body(back, current):
            rows = rows_at(steps - 1 - back)
            near = coef[rows, :]
            width = [stepd[rows, lanes] for lanes in tiles]
            pull = [grad_ssm[rows, lanes] for lanes in tiles]
            later = []
            for at, n in enumerate(names):
                leaving = column_of(near, rank + states + n)
                later.append(tuple(
                    jnp.exp2(width[t] * rate[at][t]) * (current[at][t] + pull[t] * leaving)
                    for t in range(len(tiles))
                ))
            return tuple(later)

        current = sweep(steps, body, ((zero,) * len(tiles),) * GROUP)
        for at, n in enumerate(names):
            for t, lanes in enumerate(tiles):
                decay = jnp.exp2(sums[t] * rate[at][t])
                factor, before, last = chain_pieces(decay, current[at][t], True)
                entry[0, n, :, lanes] = factor
                entry[1, n, :, lanes] = before
                total[n : n + 1, lanes] = last[:1, :]


def adjoint_kernel(rank, chips, ids, stepd, drive, grad, coef, rates, entry, kept, early, late,
                   late_total, conv_out, stepsize, dt_pre, skip, dt_weight, grad_norm2, grad_router,
                   *rest):
    sums, totals = rest[:chips], rest[chips : 2 * chips]
    (partial, grad_direct, grad_dt_pre, grad_decay, grad_dt_bias, held_sums, held, kept_here,
     in_terms, out_terms, grad_push, grad_width, sems) = rest[2 * chips :]
    core, here = ids[2], ids[3]
    states, channels = rates.shape
    length = stepd.shape[0]
    steps = length // SEGMENTS
    copies = [
        pltpu.make_async_copy(kept.at[slab], kept_here.at[slab], sems.at[slab])
        for slab in range(states // GROUP)
    ]
    for copy in copies:
        copy.start()
    for key in range(chips):
        held_sums[key] = sums[key][states : states + 1, :]
        held[key] = totals[key][...]
    state = jnp.zeros((states, channels), jnp.float32)
    for chip in reversed(range(chips)):
        grown = held[here ^ chip] + jnp.exp(held_sums[here ^ chip] * rates[...]) * state
        state = jnp.where(chip > here, grown, state)
    inner = late_total[...] + jnp.exp(late[states : states + 1, :] * rates[...]) * state
    final = jnp.where(core == 1, state, inner)
    zero = jnp.zeros((SEGMENTS, LANES), jnp.float32)
    tiles = [slice(at, at + LANES) for at in range(0, channels, LANES)]
    for group in range(0, states, GROUP):
        names = range(group, group + GROUP)
        slab = group // GROUP
        rate = [[spread(rates[n : n + 1, lanes]) for lanes in tiles] for n in names]
        current = tuple(
            tuple(
                entry[0, n, :, lanes] * final[n : n + 1, lanes] + entry[1, n, :, lanes]
                for lanes in tiles
            )
            for n in names
        )
        copies[slab].wait()

        def body(back, carry):
            current, slopes = carry
            step = steps - 1 - back
            rows = rows_at(step)
            near = coef[rows, :]
            width = [stepd[rows, lanes] for lanes in tiles]
            push = [drive[rows, lanes] for lanes in tiles]
            pull = [grad[rows, lanes] for lanes in tiles]
            later, slope = [], []
            total, width_total = [None] * len(tiles), [None] * len(tiles)
            for at, n in enumerate(names):
                entering, leaving = column_of(near, rank + n), column_of(near, rank + states + n)
                new, turned, in_term, out_term = [], [], None, None
                for t, lanes in enumerate(tiles):
                    adjoint = leaving * pull[t] + current[at][t]
                    decayed = jnp.exp2(width[t] * (rate[at][t] * LOG2E)) * adjoint
                    through = decayed * kept_here[slab, step, at, :, lanes]
                    term, rated = adjoint * entering, through * rate[at][t]
                    total[t] = term if total[t] is None else total[t] + term
                    width_total[t] = rated if width_total[t] is None else width_total[t] + rated
                    new.append(decayed)
                    turned.append(slopes[at][t] + through * width[t])
                    term = adjoint * push[t]
                    in_term = term if in_term is None else in_term + term
                    term = kept_here[slab, step + 1, at, :, lanes] * pull[t]
                    out_term = term if out_term is None else out_term + term
                place = slice(n * LANES, (n + 1) * LANES)
                in_terms[rows, place] = in_term
                out_terms[rows, place] = out_term
                later.append(tuple(new))
                slope.append(tuple(turned))
            for t, lanes in enumerate(tiles):
                add_to(grad_push, group == 0, rows, lanes, total[t])
                add_to(grad_width, group == 0, rows, lanes, width_total[t])
            return tuple(later), tuple(slope)

        none = ((zero,) * len(tiles),) * GROUP
        _, slopes = sweep(steps, body, (current, none))
        for at, n in enumerate(names):
            for t, lanes in enumerate(tiles):
                grad_decay[n : n + 1, lanes] = rates[n : n + 1, lanes] * jnp.sum(
                    slopes[at][t], axis=0, keepdims=True
                )
    pushed = grad_push[...]
    grads = (pushed * conv_out[...] + grad_width[...]) * sigmoid(dt_pre[...])
    grad_dt_pre[...] = grads
    grad_dt_bias[...] = jnp.sum(grads, axis=0, keepdims=True)
    grad_direct[...] = pushed * stepsize[...] + skip[...][None] * grad[...]
    partial[:rank, :] = product(dt_weight[...], grads, (1, 1))
    shape = (2 * states, states * LANES)
    column = lax.broadcasted_iota(jnp.int32, shape, 0)
    owner = lax.broadcasted_iota(jnp.int32, shape, 1) // LANES
    total = None
    for terms, base in ((in_terms, 0), (out_terms, states)):
        ones = jnp.where(owner + base == column, 1.0, 0.0).astype(jnp.bfloat16)
        for part in two_parts(terms[...]):
            term = once(ones, part, (1, 1))
            total = term if total is None else total + term
    cols = rank + 2 * states
    partial[rank:cols, :] = total
    row = cols
    for shared in (grad_norm2, grad_router):
        for at in range(0, shared.shape[1], length):
            partial[row : row + shared.shape[0], :] = shared[:, at : at + length]
            row += shared.shape[0]
    partial[row:, :] = jnp.zeros((partial.shape[0] - row, length), jnp.float32)


def conv_back_kernel(experts, ids, p0, p1, p2, p3, xproj_t, grad_direct, mixed, conv_out, extended,
                     marks, conv_weight, coef, grad_dt_pre, grad_decay, grad_dt_bias, grad_skip,
                     normed, halo_normed, keep, send, grad_conv, grad_halo,
                     small, grad_extended, summed, weights):
    taps, channels = conv_weight.shape
    cols, states = xproj_t.shape[0], grad_decay.shape[0]
    rank = cols - 2 * states
    length = mixed.shape[0]
    lead = (taps - 1) * SEGMENTS
    summed[...] = (p0[...] + p1[...]) + (p2[...] + p3[...])
    projected = two_parts(summed[:cols, :])
    grad_out = grad_direct[...] + product(projected, xproj_t[...], (0, 0))
    value = mixed[...]
    value_sigmoid = sigmoid(value)
    grad_mixed = grad_out * (value_sigmoid * (1.0 + value * (1.0 - value_sigmoid)))
    grad_extended[...] = jnp.zeros_like(grad_extended)
    first_tap = cols + rank + states
    small[first_tap:, :] = jnp.zeros((small.shape[0] - first_tap, channels), jnp.float32)
    for k in range(taps):
        first = (taps - 1 - k) * SEGMENTS
        masked = grad_mixed * marks[:, k : k + 1]
        small[first_tap + k : first_tap + k + 1, :] = jnp.sum(
            masked * extended[first : first + length, :], axis=0, keepdims=True
        )
        grad_extended[first : first + length, :] += conv_weight[k : k + 1, :] * masked
    grad_conv[...] = grad_extended[lead:, :]
    grad_halo[...] = jnp.zeros_like(grad_halo)
    place = lax.broadcasted_iota(jnp.int32, (SEGMENTS, channels), 0)
    for m in range(taps - 1):
        rows = grad_extended[m * SEGMENTS : (m + 1) * SEGMENTS, :]
        at = SEGMENTS - taps + 1 + m
        grad_halo[at : at + 1, :] = rows[:1, :]
        inside = jnp.where(place == SEGMENTS - 1, 0.0, pltpu.roll(rows, SEGMENTS - 1, 0))
        ends = slice(length - lead + m * SEGMENTS, length - lead + (m + 1) * SEGMENTS)
        grad_conv[ends, :] += inside
    small[:cols, :] = product(projected, conv_out[...])
    low = product(coef[...], grad_dt_pre[...], (0, 0))
    small[cols : cols + rank, :] = low[:rank, :]
    small[cols + rank : first_tap, :] = grad_decay[...]
    last = first_tap + taps
    small[last : last + 1, :] = jnp.sum(grad_mixed, axis=0, keepdims=True)
    small[last + 1 : last + 2, :] = grad_dt_bias[...]
    small[last + 2 : last + 3, :] = grad_skip[...]
    first, row = last + 3, cols
    for count in (1, experts):
        for at in range(0, 2 * channels, length):
            value = summed[row : row + count, :]
            end = at + length
            for piece in range(at // channels, -(-end // channels)):
                low, high = max(at, piece * channels), min(end, (piece + 1) * channels)
                target = first + piece * count
                small[target : target + count, low - piece * channels : high - piece * channels] = (
                    value[:, low - at : high - at]
                )
            row += count
        first += 2 * count
    weights[...] = product(normed[...], grad_conv[...], (0, 0)) + product(
        halo_normed[...], grad_halo[...], (0, 0)
    )
    in_order(ids[1], (weights, small), keep, send)


def tokens_kernel(ids, grad_conv, grad_halo, conv_high, conv_low, gate_part, rows, halo_rows,
                  slices, whole):
    weight = conv_high[...], conv_low[...]
    length = grad_conv.shape[0]
    grad = product(grad_conv[...], weight, (1, 1)) + gate_part[...]
    before = product(grad_halo[...], weight, (1, 1))
    value, value_before = rows[...], halo_rows[...]
    whole[:length, :] = grad
    whole[length:, :] = jnp.zeros((whole.shape[0] - length, whole.shape[1]), jnp.float32)
    whole[length : length + SEGMENTS, :] = before
    whole[length : length + 1, :] = jnp.sum(
        value * inverse_rms(value) * grad, axis=0, keepdims=True
    ) + jnp.sum(value_before * inverse_rms(value_before) * before, axis=0, keepdims=True)
    cut_slices(ids[0], whole, slices)


def early_weights_kernel(ids, gated, grad_hidden, normed, grad_gate_in, keep, send, whole,
                         gate):
    channels = gated.shape[1]
    halves = product(gated[...], grad_hidden[...], (0, 0))
    whole[:channels, :] = halves[:, :channels]
    whole[channels:, :] = halves[:, channels:]
    gate[...] = product(normed[...], grad_gate_in[...], (0, 0))
    in_order(ids[1], (whole, gate), keep, send)


def in_order(me, wholes, keep, send):
    count = 2 * keep.shape[0]
    levels = count.bit_length() - 1
    for place in range(count):
        block = reversed_bits(place, levels) ^ me
        out, at = (keep, place) if place < count // 2 else (send, place - count // 2)
        first = 0
        for whole in wholes:
            rows = whole.shape[0] // count
            from_row = pl.multiple_of(block * rows, 8)
            out[at, first : first + rows, :] = whole[pl.ds(from_row, rows), :]
            first += rows


def gate_tokens_kernel(ids, grad_gate_in, gate_high, gate_low, out):
    out[...] = product(grad_gate_in[...], (gate_high[...], gate_low[...]), (1, 1))


def extra_kernel(ids, p0, p1, p2, p3, extra, norm1, held, whole):
    join_slices(ids[0], (p0, p1, p2, p3), held, whole)
    row = whole.shape[0] - 2 * SEGMENTS
    channels = norm1.shape[2]
    extra[...] = whole[row : row + SEGMENTS, :]
    norm1[...] = jnp.zeros_like(norm1)
    for piece in range(whole.shape[1] // channels):
        lanes = slice(piece * channels, (piece + 1) * channels)
        norm1[0, piece : piece + 1, :] = whole[row : row + 1, lanes]


def grad_tokens_kernel(taps, ids, p0, p1, p2, p3, from_next, rows, gain, grad_hidden, out,
                       held, whole, tiles):
    join_slices(ids[0], (p0, p1, p2, p3), held, whole)
    length = rows.shape[0]
    lead = (taps - 1) * SEGMENTS
    for m in range(taps - 1):
        row = length - lead + (m + 1) * SEGMENTS - 1
        at = SEGMENTS - taps + 1 + m
        whole[row : row + 1, :] += from_next[at : at + 1, :]
    value = rows[...]
    whole[:length, :] = (
        norm_back(value, inverse_rms(value), gain[...][None], whole[:length, :]) + grad_hidden[...]
    )
    deinterleave_to(whole, tiles, out)


def early_out_kernel(ids, summed, out_weight):
    count, rows, channels = summed.shape
    levels = count.bit_length() - 1
    for block in range(count):
        value = summed[reversed_bits(block ^ ids[1], levels)]
        half, row = divmod(block * rows, channels)
        out_weight[row : row + rows, half * channels : (half + 1) * channels] = value


def weights_out_kernel(counts, ids, early, late, norm1, weight, *rest):
    *outs, sum_norm1, small = rest
    count, rows = early.shape[0], early.shape[1]
    more = late.shape[1] - rows
    levels = count.bit_length() - 1
    for block in range(count):
        place = reversed_bits(block ^ ids[1], levels)
        small[block * more : (block + 1) * more, :] = late[place, rows:, :]
        weight[block * rows : (block + 1) * rows, 0, :] = late[place, :rows, :]
        weight[block * rows : (block + 1) * rows, 1, :] = early[place]
    first = 0
    channels = small.shape[1]
    for out, used in zip(outs, counts):
        per = out.shape[-1] // channels
        each = used // per
        for piece in range(per):
            lanes = slice(piece * channels, (piece + 1) * channels)
            if len(out.shape) == 1:
                out[lanes] = small[first, :]
            else:
                out[:, lanes] = small[first : first + each, :]
            first += each
    for piece in range(sum_norm1.shape[0] // channels):
        sum_norm1[piece * channels : (piece + 1) * channels] = norm1[0, piece, :]


def local(
    tokens, norm1_gain, in_weight, conv_weight, conv_bias, xproj_weight, dt_weight, dt_bias,
    decay_log, skip_gain, out_weight, norm2_gain, router_weight, expert_in, expert_out,
    segments, expert_ids, cotangent,
):
    length, width = tokens.shape
    taps, channels = conv_weight.shape
    experts = router_weight.shape[1]
    wide = experts
    capacity = 5 * length // (4 * experts)
    states, rank = decay_log.shape[0], dt_weight.shape[0]
    chips = wide // 2
    slots = chips * capacity
    steps = length // SEGMENTS
    me_wide = lax.axis_index("wide")
    ids = jnp.stack([lax.axis_index("narrow"), me_wide, me_wide & 1, me_wide // 2]).astype(jnp.int32)
    half, double = length // 2, width // 2
    bf16 = jnp.bfloat16
    rows_shape, channel_rows = shape_of(length, width), shape_of(length, channels)
    packed, packed_slots = shape_of(half, double), shape_of(slots, double)
    vmem = lambda *shape: pltpu.VMEM(shape, jnp.float32)
    xproj_t, router_t = xproj_weight.T, router_weight.T
    cols = xproj_t.shape[0]

    tiled = vmem(width // LANES, length, LANES)

    halo_rows = wide_shift(tokens[length - SEGMENTS :], 1)

    (marks, slots_own, slots_other, rows_own, rows_other, rows_slice, cot_slice, cot_own,
     cot_other, conv_high, conv_low, gate_high, gate_low) = call(
        functools.partial(start_kernel, capacity),
        [shape_of(length, SEGMENTS)]
        + [shape_of(slots, length, dtype=bf16)] * 2
        + [shape_of(length, slots, dtype=bf16)] * 2
        + [packed, packed, packed_slots, packed_slots]
        + [shape_of(width, channels, dtype=bf16)] * 4,
        ids, segments.reshape(-1, LANES), expert_ids.reshape(1, length), tokens, cotangent,
        in_weight,
        scratch=[pltpu.VMEM((segments.shape[0] // LANES, LANES), jnp.int32),
                 pltpu.VMEM((1, length), jnp.int32)] + [vmem(length, width)] * 2
        + [vmem(width, 2, channels), vmem(length, width), tiled, vmem(2, width, channels),
           pltpu.SemaphoreType.DMA((5,))],
        far_in=[0, 1, 2, 3, 4],
    )
    cot_pair = cot_own + core_swap(cot_other)
    rows, normed, conv_in, gate_in = call(
        front_kernel,
        [rows_shape, rows_shape, channel_rows, channel_rows],
        ids, tokens, norm1_gain, conv_high, conv_low, gate_high, gate_low,
        scratch=[tiled],
    )
    mixed, conv_out, partial, extended, halo_normed = call(
        conv_kernel,
        [channel_rows, channel_rows, shape_of(cols, length),
         shape_of(length + (taps - 1) * SEGMENTS, channels), shape_of(SEGMENTS, width)],
        ids, halo_rows, norm1_gain, conv_high, conv_low, conv_in, marks, conv_weight,
        conv_bias, xproj_t, after=[cot_pair],
    )
    partials = narrow_all(partial)

    partials = narrow_all(partial)

    cot_blocks = chip_each(hold(cot_pair, partial), chips)

    entry_shape = shape_of(2, states, SEGMENTS, channels)
    total_rows = -(-(states + 1) // 8) * 8
    coef, dt_pre, stepsize, drive, stepd, rates, entry, total = call(
        totals_kernel,
        [shape_of(length, LANES)] + [channel_rows] * 4
        + [shape_of(states, channels), entry_shape, shape_of(total_rows, channels)],
        ids, *partials, dt_weight, dt_bias, decay_log, conv_out, marks,
        scratch=[vmem(LANES, channels)],
    )
    total_shape = shape_of(total_rows, channels)
    early, late, chip_total = call(
        pair_kernel, [total_shape] * 3, ids, total, core_swap(total), rates, after=[cot_blocks]
    )
    chip_totals = chip_all(chip_total, chips)
    slabs = states // GROUP
    cot_held = hold(cot_blocks, chip_total)
    cot_one, cot_two = narrow_swap(cot_held, 1), narrow_swap(cot_held, 2)
    kept_shape = (slabs, steps + 1, GROUP, SEGMENTS, channels)
    ssm_skip, gated, mixer_slices, kept = call(
        functools.partial(states_kernel, rank),
        [channel_rows, channel_rows, shape_of(4, half, double), shape_of(*kept_shape)],
        ids, stepd, drive, coef, rates, entry, early, conv_out, gate_in, skip_gain,
        out_weight, *chip_totals,
        scratch=[vmem(chips, total_rows, channels), vmem(length, width), vmem(*kept_shape),
                 pltpu.SemaphoreType.DMA((slabs,))],
        out_place=[3],
    )
    mixer_slices = hold(mixer_slices, cot_one, cot_two)
    expert_rows, square = shape_of(2 * slots, width), (expert_in.shape[1], expert_in.shape[2])
    hidden_units = square[1]
    hidden_slice, hidden_own, hidden_other = call(
        dispatch_kernel,
        [packed, packed_slots, packed_slots],
        ids, *narrow_each(mixer_slices), rows_slice, slots_own, slots_other,
    )
    hidden_blocks = chip_each(hidden_own + core_swap(hidden_other), chips)
    upper, lower = hold(cot_one[: slots // 2], hidden_own), hold(cot_two[slots // 2 :], hidden_own)
    cot_three = jnp.concatenate([narrow_swap(upper, 2), narrow_swap(lower, 1)])
    raw, cot, in_high, in_low, out_high, out_low = call(
        raw_kernel,
        [shape_of(2 * slots, hidden_units), expert_rows]
        + [shape_of(*square, dtype=bf16)] * 2
        + [shape_of(square[1], square[0], dtype=bf16)] * 2,
        ids, cot_blocks, cot_one, cot_two, cot_three, expert_in[0], expert_out[0],
        scratch=[vmem(4, slots, double)],
    )
    hidden_parts = lax.all_gather(hold(hidden_blocks, raw), "narrow")
    slices_shape = shape_of(4, slots, double)
    grad_slices, second, act, grad_pre, gates, grad_logits, grad_norm2 = call(
        expert_kernel,
        [slices_shape, expert_rows] + [shape_of(2 * slots, hidden_units)] * 2
        + [shape_of(2 * slots, 1), shape_of(2 * slots, experts), shape_of(1, width)],
        ids, hidden_parts, raw, in_high, in_low, norm2_gain, router_t,
        scratch=[vmem(2 * slots, width)],
    )
    grad_mine = pair_sum(narrow_each(grad_slices))
    value_slices, grad_expert_in, grad_expert_out, grad_router_t = call(
        expert_rest_kernel,
        [slices_shape, shape_of(*square), shape_of(square[1], square[0]),
         shape_of(experts, width)],
        ids, second, act, grad_pre, gates, grad_logits, cot, out_high, out_low,
        scratch=[vmem(2 * slots, width)],
    )
    grad_back = chip_each(grad_mine, chips)
    value_mine = pair_sum(narrow_each(value_slices))
    grad_slice = call(
        home_kernel, [packed], ids, grad_back, core_swap(grad_back), cot_slice, rows_own,
        rows_other, after=[value_mine],
    )[0]
    grad_parts = narrow_all(grad_slice)
    value_back = chip_each(value_mine, chips)

    def whole_of(parts, after=()):
        return call(
            whole_kernel, [rows_shape], ids, *parts, after=after,
            scratch=[vmem(4, half, double), vmem(length, width), tiled],
        )[0]

    grad_hidden, grad_ssm, grad_gate_in, grad_skip, back_entry, back_total = call(
        functools.partial(leaving_kernel, rank),
        [rows_shape, channel_rows, channel_rows, shape_of(1, channels), entry_shape,
         shape_of(states, channels)],
        ids, *grad_parts, out_weight, gate_in, ssm_skip, conv_out, stepd, coef, rates,
        scratch=[vmem(4, half, double)], after=[value_back],
    )
    other_back = core_swap(back_total)
    block = width // wide
    half_blocks = shape_of(wide // 2, 2 * block, channels)
    early_keep, early_send = call(
        early_weights_kernel,
        [half_blocks, half_blocks],
        ids, gated, grad_hidden, normed, grad_gate_in,
        scratch=[vmem(width, channels)] * 2,
    )
    back_late, back_chip = call(
        pair_back_kernel, [shape_of(states, channels)] * 2,
        ids, back_total, other_back, early, rates, after=[early_keep],
    )
    back_totals = chip_all(back_chip, chips)
    early_arrived = core_swap(hold(early_send, back_chip))
    out_sum, gate_sum = (
        WideSum(early_keep[:, rows], early_send[:, rows])
        for rows in (slice(0, block), slice(block, None))
    )
    out_sum.arrived, gate_sum.arrived = early_arrived[:, :block], early_arrived[:, block:]
    out_sum.finish()
    gate_sum.finish()
    first_step = out_sum.start(*back_totals)

    shared_rows = (experts + 1) * (width // length)
    partial_rows = cols + shared_rows + -(cols + shared_rows) % 8
    partial_back, grad_direct, grad_dt_pre, grad_decay, grad_dt_bias = call(
        functools.partial(adjoint_kernel, rank, chips),
        [shape_of(partial_rows, length), channel_rows, channel_rows, shape_of(states, channels),
         shape_of(1, channels)],
        ids, stepd, drive, grad_ssm, coef, rates, back_entry, kept, early, late, back_late,
        conv_out, stepsize, dt_pre, skip_gain, dt_weight, grad_norm2, grad_router_t,
        *chip_totals, *back_totals,
        scratch=[vmem(chips, 1, channels), vmem(chips, states, channels), vmem(*kept_shape),
                 vmem(length, states * LANES), vmem(length, states * LANES),
                 vmem(length, channels), vmem(length, channels),
                 pltpu.SemaphoreType.DMA((slabs,))],
        in_place=[6], after=[out_sum.send, gate_sum.send],
    )
    partials_back = narrow_all(partial_back)
    gate_part = call(
        gate_tokens_kernel, [rows_shape], ids, grad_gate_in, gate_high, gate_low,
        after=[partial_back],
    )[0]
    out_sum.finish(partial_back)
    out_sum.start()
    gate_sum.start(partial_back)
    grain = 8 * wide
    small_rows = cols + rank + states + taps + 3 + (experts + 1) * (width // channels)
    small_rows += -small_rows % grain
    more = small_rows // wide
    half_blocks = shape_of(wide // 2, block + more, channels)
    token_rows = length + 2 * SEGMENTS
    conv_keep, conv_send, grad_conv, grad_halo = call(
        functools.partial(conv_back_kernel, experts),
        [half_blocks, half_blocks, channel_rows, shape_of(SEGMENTS, channels)],
        ids, *partials_back, xproj_t, grad_direct, mixed, conv_out, extended, marks,
        conv_weight, coef, grad_dt_pre, grad_decay, grad_dt_bias, grad_skip,
        normed, halo_normed,
        scratch=[vmem(small_rows, channels),
                 vmem(length + (taps - 1) * SEGMENTS, channels), vmem(partial_rows, length),
                 vmem(width, channels)],
        after=[gate_sum.arrived, out_sum.arrived],
    )
    (token_slices,) = call(
        tokens_kernel, [shape_of(4, token_rows // 2, double)],
        ids, grad_conv, grad_halo, conv_high, conv_low, gate_part, rows, halo_rows,
        scratch=[vmem(token_rows, width)],
    )
    out_sum.finish()
    gate_sum.finish()
    conv_sum = WideSum(conv_keep, conv_send)
    conv_sum.start()
    conv_sum.finish()
    (output_slice,) = call(
        home_kernel, [packed], ids, value_back, core_swap(hold(value_back, conv_keep)),
        hidden_slice, rows_own, rows_other,
    )
    levels = len(conv_sum.swaps)

    def extra_of(parts):
        return call(
            extra_kernel,
            [shape_of(SEGMENTS, width), shape_of(1, SEGMENTS, channels)],
            ids, *parts,
            scratch=[vmem(4, token_rows // 2, double), vmem(token_rows, width)],
        )

    def grad_tokens_of(parts, from_next):
        return call(
            functools.partial(grad_tokens_kernel, taps),
            [rows_shape], ids, *parts, from_next, rows, norm1_gain, grad_hidden,
            scratch=[vmem(4, token_rows // 2, double), vmem(token_rows, width), tiled],
        )[0]

    def out_weight_of(total, *others):
        return call(
            early_out_kernel, [shape_of(channels, width)], ids, total, after=others
        )[0]

    if levels == 3:
        sums = conv_sum, gate_sum, out_sum
        joint = [conv_sum.start(), *start_both(gate_sum, out_sum)]
        token_each = narrow_each(token_slices)
        for part in sums:
            part.finish(*joint, *token_each, output_slice)
        joint = [*start_both(conv_sum, gate_sum), out_sum.start()]
        token_parts = narrow_all(pair_sum(token_each))
        extra, norm1 = extra_of(token_parts)
        from_next = wide_shift(extra, -1)
        for part in sums:
            part.finish(*joint, norm1, from_next)
        arrived, norm1_other = conv_sum.start_with(norm1)
        joint = [arrived, gate_sum.start()]
        output_parts = narrow_all(hold(output_slice, norm1))
        for part in sums[:2]:
            part.finish(*joint, *output_parts)
        norm1 = norm1 + norm1_other
        arrived, norm1_other = conv_sum.start_with(norm1)
        grad_tokens = grad_tokens_of(token_parts, from_next)
        joint = [arrived, *start_both(gate_sum, out_sum, grad_tokens)]
        output = whole_of(output_parts, after=[conv_sum.send])
        for part in sums:
            part.finish(*joint, output, grad_tokens)
        norm1 = norm1 + norm1_other
        arrived, norm1_other = conv_sum.start_with(norm1)
        sum_out_weight = out_weight_of(out_sum.keep, conv_sum.send)
        conv_sum.finish(sum_out_weight)
        norm1 = norm1 + norm1_other
    else:
        token_parts = narrow_all(pair_sum(narrow_each(token_slices)))
        extra, norm1 = extra_of(token_parts)
        grad_tokens = grad_tokens_of(token_parts, wide_shift(extra, -1))
        output = whole_of(narrow_all(output_slice))
        sum_out_weight = out_weight_of(out_sum.rest())
        norm1 = norm1 + core_swap(norm1)
        norm1 = pair_sum(chip_all(norm1, chips))
    per = width // channels
    counts = (cols, rank, states, taps, 1, 1, 1, per, per * experts)
    (weight_sum, sum_xproj_t, sum_dt_weight, sum_decay, sum_taps, sum_conv_bias, sum_dt_bias,
     sum_skip, sum_norm2, sum_router_t, sum_norm1) = call(
        functools.partial(weights_out_kernel, counts),
        [shape_of(width, 2, channels)]
        + [shape_of(rows, channels) for rows in (cols, rank, states, taps)]
        + [shape_of(channels)] * 3
        + [shape_of(width), shape_of(experts, width), shape_of(width)],
        ids, gate_sum.rest(), conv_sum.rest(), norm1, scratch=[vmem(small_rows, channels)],
    )
    return (
        output,
        grad_tokens,
        sum_norm1,
        weight_sum,
        sum_taps,
        sum_conv_bias,
        sum_xproj_t.T,
        sum_dt_weight,
        sum_dt_bias,
        sum_decay,
        sum_skip,
        sum_out_weight,
        sum_norm2,
        sum_router_t.T,
        grad_expert_in[None],
        grad_expert_out[None],
    )


def solution(mesh):
    in_specs = (
        P("wide", None),
        P(),
        P(None, None, "narrow"),
        P(None, "narrow"),
        P("narrow"),
        P("narrow", None),
        P(None, "narrow"),
        P("narrow"),
        P(None, "narrow"),
        P("narrow"),
        P("narrow", None),
        P(),
        P(),
        P("wide", None, "narrow"),
        P("wide", "narrow", None),
        P(),
        P("wide", None),
        P("wide", None),
    )
    out_specs = (
        P("wide", None),
        P("wide", None),
        P(),
        P(None, None, "narrow"),
        P(None, "narrow"),
        P("narrow"),
        P("narrow", None),
        P(None, "narrow"),
        P("narrow"),
        P(None, "narrow"),
        P("narrow"),
        P("narrow", None),
        P(),
        P(),
        P("wide", None, "narrow"),
        P("wide", "narrow", None),
    )
    return jax.shard_map(local, mesh=mesh, in_specs=in_specs, out_specs=out_specs, check_vma=False)
```

profile of v0, /device:TPU:0, one launch (start us, length us, event | category | flops | bytes accessed | tf_op | source)
XLA Modules:
  0.0 229.6 jit_solution(12382218772850182092)
XLA Ops:
  0.7 4.5 %shard_map.297 = (f32[256,8]{1,0:T(8,128)S(1)}, bf16[160,256]{1,0:T(8,128)(2,1)S(1)}, bf16[160,256]{1,0:T(8,128)(2,1)S(1)}, bf16[256,160]{1,0:T(8,128)(2,1)S(1)}...) custom-call(s32[4]{0:T(128)S(1)} %pad_add_fusion.refs_0_, ...), custom_call_target="tpu_custom_call" | custom-call | flops 1 | bytes 1 | tf_op jit(solution)/shard_map/pallas_call | solution.py:46
  8.0 2.5 %shard_map.298 = (f32[256,768]{1,0:T(8,128)S(1)}, f32[256,768]{1,0:T(8,128)S(1)}, f32[256,384]{1,0:T(8,128)S(1)}, f32[256,384]{1,0:T(8,128)S(1)}) custom-call(s32[4]{0:T(128)S(1)} %pad_add_fusion.refs_0_, f32[256,768]{1,0:T(8,128)S(1)} %copy-done.1, f32[768]{0:T(1024)S(1)} %copy-done.6, bf16[768,384]{1,0:T(8,128)(2,1)S(1)} %get-tuple-element.130.refs_3_, ...), custom_call_target="tpu_custom_call" | custom-call | flops 1 | bytes 1 | tf_op jit(solution)/shard_map/pallas_call | solution.py:46
  12.1 3.0 %collective-permute-start.2 = (f32[80,256]{1,0:T(8,128)S(1)}, f32[80,256]{1,0:T(8,128)S(1)}, u32[]{:S(2)}, u32[]{:S(2)}) collective-permute-start(f32[80,256]{1,0:T(8,128)S(1)} %get-tuple-element.138.refs_1_), channel_id=1, source_target_pairs={{0,8},{8,0},{16,24},{24,16},{1,9},{9,1},{17,25},{25,17},{2,10},{10... | collective-permute-start | bytes 245768 | tf_op jit(solution)/shard_map/ppermute | solution.py:165
  18.8 2.6 %collective-permute-start.7 = (f32[40,384]{1,0:T(8,128)S(1)}, f32[40,384]{1,0:T(8,128)S(1)}, u32[]{:S(2)}, u32[]{:S(2)}) collective-permute-start(f32[40,384]{1,0:T(8,128)S(1)} %get-tuple-element.281), channel_id=1, source_target_pairs={{0,4},{1,5},{2,6},{3,7},{4,0},{5,1},{6,2},{7,3},{8,12},{9,13},{10,... | collective-permute-start | bytes 184328 | tf_op jit(solution)/shard_map/ppermute | solution.py:175
  22.5 2.6 %shard_map.300 = (f32[256,128]{1,0:T(8,128)S(1)}, f32[256,384]{1,0:T(8,128)S(1)}, f32[256,384]{1,0:T(8,128)S(1)}, f32[256,384]{1,0:T(8,128)S(1)}, f32[256,384]{1...) custom-call(s32[4]{0:T(128)S(1)} %pad_add_fusion.refs_0_, ...), custom_call_target="tpu_custom_call" | custom-call | flops 1 | bytes 1 | tf_op jit(solution)/shard_map/pallas_call | solution.py:46
  34.6 2.2 collective-permute-done.10.refs_13_.refs_20_
  38.7 4.4 %shard_map.302 = (f32[256,384]{1,0:T(8,128)S(1)}, f32[256,384]{1,0:T(8,128)S(1)}, f32[4,128,384]{2,1,0:T(8,128)S(1)}, f32[4,33,4,8,384]{4,3,2,1,0:T(8,128)S(1)}) custom-call(s32[4]{0:T(128)S(1)} %pad_add_fusion.refs_0_, f32[256,384]{1,0:T(8,128)S(1)} %get-tuple-element.140.refs_1_.refs_9_, f32[256,384]{1,0:T(8,128)S(1)} %get-tuple-element.141.refs_2_, ...), custom_call_target="tpu_custom_call" | custom-call | flops 1 | bytes 1 | tf_op jit(solution)/shard_map/pallas_call | solution.py:46
  44.3 2.4 %collective-permute-start.16 = (f32[128,384]{1,0:T(8,128)S(1)}, f32[128,384]{1,0:T(8,128)S(1)}, u32[]{:S(2)}, u32[]{:S(2)}) collective-permute-start(f32[128,384]{1,0:T(8,128)S(1)} %get-tuple-element.261), channel_id=1, source_target_pairs={{0,24},{8,16},{16,8},{24,0},{1,25},{9,17},{17,9},{25,1},{2,26},{10... | collective-permute-start | bytes 589832 | tf_op jit(solution)/shard_map/ppermute | solution.py:165
  46.7 3.3 %collective-permute-done.14.refs_2_ = f32[128,384]{1,0:T(8,128)S(1)} collective-permute-done((f32[128,384]{1,0:T(8,128)S(1)}, f32[128,384]{1,0:T(8,128)S(1)}, u32[]{:S(2)}, u32[]{:S(2)}) %collective-permute-start.14) | collective-permute-done | bytes 196640 | tf_op jit(solution)/shard_map/ppermute | solution.py:165
  50.0 2.4 %collective-permute-done.15.refs_3_ = f32[128,384]{1,0:T(8,128)S(1)} collective-permute-done((f32[128,384]{1,0:T(8,128)S(1)}, f32[128,384]{1,0:T(8,128)S(1)}, u32[]{:S(2)}, u32[]{:S(2)}) %collective-permute-start.15) | collective-permute-done | bytes 196640 | tf_op jit(solution)/shard_map/ppermute | solution.py:165
  56.1 2.3 collective-permute-start.19
  60.5 2.8 %shard_map.304 = (f32[320,768]{1,0:T(8,128)S(1)}, f32[320,768]{1,0:T(8,128)S(1)}, bf16[768,768]{1,0:T(8,128)(2,1)S(1)}, bf16[768,768]{1,0:T(8,128)(2,1)S(1)}, bf...) custom-call(s32[4]{0:T(128)S(1)} %pad_add_fusion.refs_0_, f32[160,384]{1,0:T(8,128)S(1)} %pad_maximum_fusion.11.refs_4_.refs_1_, ...), custom_call_target="tpu_custom_call" | custom-call | flops 1 | bytes 1 | tf_op jit(solution)/shard_map/pallas_call | solution.py:46
  64.5 12.9 %all-gather = f32[640,384]{1,0:T(8,128)S(1)} all-gather(f32[160,384]{1,0:T(8,128)S(1)} %pad_maximum_fusion.12), channel_id=2, replica_groups=mesh['narrow'=4,'wide'=8] {'narrow'}, dimensions={0}, use_global_device_ids=true | all-gather | bytes 1228800 | tf_op jit(solution)/shard_map/all_gather | solution.py:1133
  77.4 5.8 %shard_map.305 = (f32[4,160,384]{2,1,0:T(8,128)S(1)}, f32[320,768]{1,0:T(8,128)S(1)}, f32[320,768]{1,0:T(8,128)S(1)}, f32[320,768]{1,0:T(8,128)S(1)}, f32[320,1]...) custom-call(s32[4]{0:T(128)S(1)} %pad_add_fusion.refs_0_, f32[4,160,384]{2,1,0:T(8,128)S(1)} %bitcast.58, ...), custom_call_target="tpu_custom_call" | custom-call | flops 1 | bytes 1 | tf_op jit(solution)/shard_map/pallas_call | solution.py:46
  86.9 7.3 %shard_map.306 = (f32[4,160,384]{2,1,0:T(8,128)S(1)}, f32[768,768]{1,0:T(8,128)}, f32[768,768]{1,0:T(8,128)}, f32[8,768]{1,0:T(8,128)S(1)}) custom-call(s32[4]{0:T(128)S(1)} %pad_add_fusion.refs_0_, f32[320,768]{1,0:T(8,128)S(1)} %get-tuple-element.164.refs_1_, f32[320,768]{1,0:T(8,128)S(1)} %get-tuple-element.165.refs_2_, ...), custom_call_target="tpu_custom_call" | custom-call | flops 1 | bytes 1 | tf_op jit(solution)/shard_map/pallas_call | solution.py:46
  98.5 2.2 collective-permute-start.33
  104.3 2.5 %collective-permute-done.34 = f32[40,384]{1,0:T(8,128)S(1)} collective-permute-done((f32[40,384]{1,0:T(8,128)S(1)}, f32[40,384]{1,0:T(8,128)S(1)}, u32[]{:S(2)}, u32[]{:S(2)}) %collective-permute-start.34) | collective-permute-done | bytes 61472 | tf_op jit(solution)/shard_map/ppermute | solution.py:175
  116.3 4.2 %collective-permute-done.27 = f32[40,384]{1,0:T(8,128)S(1)} collective-permute-done((f32[40,384]{1,0:T(8,128)S(1)}, f32[40,384]{1,0:T(8,128)S(1)}, u32[]{:S(2)}, u32[]{:S(2)}) %collective-permute-start.27) | collective-permute-done | bytes 61472 | tf_op jit(solution)/shard_map/ppermute | solution.py:175
  121.7 3.3 %shard_map.308 = (f32[256,768]{1,0:T(8,128)S(1)}, f32[256,384]{1,0:T(8,128)S(1)}, f32[256,384]{1,0:T(8,128)S(1)}, f32[1,384]{1,0:T(1,128)S(1)}, f32[2,16,8,384]{3,2,1,0:T(8,128)S(1)}, /*index=5*/f32[16,384]{1,0:T(8,128)S(1)}) custom-call(s32[4]{0:T(128)S(1)} %pad_add_fusion.refs_0_, f32[128,384]{1,0:T(8,128)S(1)} %shard_map.307.refs_1_, ...), custom_call_target="tpu_custom_call" | custom-call | flops 1 | bytes 1 | tf_op jit(solution)/shard_map/pallas_call | solution.py:46
  133.8 2.7 %collective-permute-done.42.refs_25_ = f32[16,384]{1,0:T(8,128)S(1)} collective-permute-done((f32[16,384]{1,0:T(8,128)S(1)}, f32[16,384]{1,0:T(8,128)S(1)}, u32[]{:S(2)}, u32[]{:S(2)}) %collective-permute-start.42) | collective-permute-done | bytes 24608 | tf_op jit(solution)/shard_map/ppermute | solution.py:175
  136.4 7.1 %shard_map.311 = (f32[112,256]{1,0:T(8,128)S(1)}, f32[256,384]{1,0:T(8,128)S(1)}, f32[256,384]{1,0:T(8,128)S(1)}, f32[16,384]{1,0:T(8,128)S(1)}, f32[1,384]{1,0:T(1,128)S(1)}) custom-call(s32[4]{0:T(128)S(1)} %pad_add_fusion.refs_0_, f32[256,384]{1,0:T(8,128)S(1)} %get-tuple-element.140.refs_1_.refs_9_, f32[256,384]{1,0:T(8,128)S(1)} %get-tuple-element.141.refs_2_, ...), custom_call_target="tpu_custom_call" | custom-call | flops 1 | bytes 1 | tf_op jit(solution)/shard_map/pallas_call | solution.py:46
  154.1 2.7 %shard_map.312 = (f32[4,120,384]{2,1,0:T(8,128)S(1)}, f32[4,120,384]{2,1,0:T(8,128)S(1)}, f32[256,384]{1,0:T(8,128)S(1)}, f32[8,384]{1,0:T(8,128)S(1)}) custom-call(s32[4]{0:T(128)S(1)} %pad_add_fusion.refs_0_, f32[112,256]{1,0:T(8,128)S(1)} %get-tuple-element.196.refs_1_.refs_4_, f32[112,256]{1,0:T(8,128)S(1)} %collective-permute-done.44.refs_2_, ...), custom_call_target="tpu_custom_call" | custom-call | flops 1 | bytes 1 | tf_op jit(solution)/shard_map/pallas_call | solution.py:46
  157.0 2.7 %collective-permute-start.62 = (f32[1,192,384]{2,1,0:T(8,128)S(1)}, f32[1,192,384]{2,1,0:T(8,128)S(1)}, u32[]{:S(2)}, u32[]{:S(2)}) collective-permute-start(f32[1,192,384]{2,1,0:T(8,128)S(1)} %pad_maximum_fusion.8), channel_id=1, source_target_pairs={{0,4},{1,5},{2,6},{3,7},{4,0},{5,1},{6,2},{7,3},{8,12},{9,13},{10,... | collective-permute-start | bytes 884744 | tf_op jit(solution)/shard_map/ppermute | solution.py:175
  167.9 5.8 %collective-permute-done.62 = f32[1,192,384]{2,1,0:T(8,128)S(1)} collective-permute-done((f32[1,192,384]{2,1,0:T(8,128)S(1)}, f32[1,192,384]{2,1,0:T(8,128)S(1)}, u32[]{:S(2)}, u32[]{:S(2)}) %collective-permute-start.62) | collective-permute-done | bytes 294944 | tf_op jit(solution)/shard_map/ppermute | solution.py:175
  174.1 5.6 %collective-permute-done.61 = f32[2,120,384]{2,1,0:T(8,128)S(1)} collective-permute-done((f32[2,120,384]{2,1,0:T(8,128)S(1)}, f32[2,120,384]{2,1,0:T(8,128)S(1)}, u32[]{:S(2)}, u32[]{:S(2)}) %collective-permute-start.61) | collective-permute-done | bytes 368672 | tf_op jit(solution)/shard_map/ppermute | solution.py:175
  185.6 4.6 %collective-permute-done.54.refs_2_ = f32[136,384]{1,0:T(8,128)S(1)} collective-permute-done((f32[136,384]{1,0:T(8,128)S(1)}, f32[136,384]{1,0:T(8,128)S(1)}, u32[]{:S(2)}, u32[]{:S(2)}) %collective-permute-start.54) | collective-permute-done | bytes 208928 | tf_op jit(solution)/shard_map/ppermute | solution.py:165
  190.3 3.5 %collective-permute-done.55.refs_3_ = f32[136,384]{1,0:T(8,128)S(1)} collective-permute-done((f32[136,384]{1,0:T(8,128)S(1)}, f32[136,384]{1,0:T(8,128)S(1)}, u32[]{:S(2)}, u32[]{:S(2)}) %collective-permute-start.55) | collective-permute-done | bytes 208928 | tf_op jit(solution)/shard_map/ppermute | solution.py:165
  204.1 2.7 %shard_map.318 = f32[256,768]{1,0:T(8,128)} custom-call(s32[4]{0:T(128)S(1)} %pad_add_fusion.refs_0_, f32[136,384]{1,0:T(8,128)S(1)} %add_add_fusion.refs_1_, f32[136,384]{1,0:T(8,128)S(1)} %collective-permute-done.54.refs_2_, f32[136,384]{1,0:T(8,128)S(1)} %collective-permute-done.55.refs_3_, f32[136,384]{1,0:T(8,128)S(1)} %collective-permute-done.56.refs_4_, ...), custom_call_target="tpu_custom_call" | custom-call | flops 1 | bytes 1 | tf_op jit(solution)/shard_map/pallas_call | solution.py:46
  206.8 3.2 %collective-permute-done.66 = f32[1,128,384]{2,1,0:T(8,128)S(1)} collective-permute-done((f32[1,128,384]{2,1,0:T(8,128)S(1)}, f32[1,128,384]{2,1,0:T(8,128)S(1)}, u32[]{:S(2)}, u32[]{:S(2)}) %collective-permute-start.66) | collective-permute-done | bytes 196640 | tf_op jit(solution)/shard_map/ppermute | solution.py:175
  210.0 2.5 %collective-permute-done.58.refs_3_ = f32[128,384]{1,0:T(8,128)S(1)} collective-permute-done((f32[128,384]{1,0:T(8,128)S(1)}, f32[128,384]{1,0:T(8,128)S(1)}, u32[]{:S(2)}, u32[]{:S(2)}) %collective-permute-start.58) | collective-permute-done | bytes 196640 | tf_op jit(solution)/shard_map/ppermute | solution.py:165
  216.8 7.3 %collective-permute-done.69 = f32[1,248,384]{2,1,0:T(8,128)S(1)} collective-permute-done((f32[1,248,384]{2,1,0:T(8,128)S(1)}, f32[1,248,384]{2,1,0:T(8,128)S(1)}, u32[]{:S(2)}, u32[]{:S(2)}) %collective-permute-start.69) | collective-permute-done | bytes 380960 | tf_op jit(solution)/shard_map/ppermute | solution.py:175
  226.8 2.5 %shard_map.320 = (f32[768,2,384]{2,1,0:T(2,128)}, f32[80,384]{1,0:T(8,128)}, f32[48,384]{1,0:T(8,128)}, f32[16,384]{1,0:T(8,128)}, f32[4,384]{1,0:T(4,128)}, /*i...) custom-call(s32[4]{0:T(128)S(1)} %pad_add_fusion.refs_0_, ...), custom_call_target="tpu_custom_call" | custom-call | flops 1 | bytes 1 | tf_op jit(solution)/shard_map/pallas_call | solution.py:46
  (216 shorter events, 101.7 us)
Async XLA Ops:
  12.1 9.3 %collective-permute-start.2 = (f32[80,256]{1,0:T(8,128)S(1)}, f32[80,256]{1,0:T(8,128)S(1)}, u32[]{:S(2)}, u32[]{:S(2)}) collective-permute-start(f32[80,256]{1,0:T(8,128)S(1)} %get-tuple-element.138.refs_1_), channel_id=1, source_target_pairs={{0,8},{8,0},{16,24},{24,16},{1,9},{9,1},{17,25},{25,17},{2,10},{10... | collective-permute-start | bytes 245768 | tf_op jit(solution)/shard_map/ppermute | solution.py:165
  16.6 8.5 %collective-permute-start.6 = (f32[40,384]{1,0:T(8,128)S(1)}, f32[40,384]{1,0:T(8,128)S(1)}, u32[]{:S(2)}, u32[]{:S(2)}) collective-permute-start(f32[40,384]{1,0:T(8,128)S(1)} %get-tuple-element.282), channel_id=1, source_target_pairs={{0,2},{1,3},{2,0},{3,1},{4,6},{5,7},{6,4},{7,5},{8,10},{9,11},{10,... | collective-permute-start | bytes 184328 | tf_op jit(solution)/shard_map/ppermute | solution.py:175
  28.1 15.0 %collective-permute-start.12 = (f32[160,384]{1,0:T(8,128)S(1)}, f32[160,384]{1,0:T(8,128)S(1)}, u32[]{:S(2)}, u32[]{:S(2)}) collective-permute-start(f32[160,384]{1,0:T(8,128)S(1)} %pad_maximum_fusion.11.refs_4_.refs_1_), channel_id=1, source_target_pairs={{0,8},{8,0},{16,24},{24,16},{1,9},{9,1},{17,25},{25,17},{2,10},{10... | collective-permute-start | bytes 737288 | tf_op jit(solution)/shard_map/ppermute | solution.py:165
  29.6 13.5 %collective-permute-start.13 = (f32[160,384]{1,0:T(8,128)S(1)}, f32[160,384]{1,0:T(8,128)S(1)}, u32[]{:S(2)}, u32[]{:S(2)}) collective-permute-start(f32[160,384]{1,0:T(8,128)S(1)} %pad_maximum_fusion.11.refs_4_.refs_1_), channel_id=1, source_target_pairs={{0,16},{8,24},{16,0},{24,8},{1,17},{9,25},{17,1},{25,9},{2,18},{10... | collective-permute-start | bytes 737288 | tf_op jit(solution)/shard_map/ppermute | solution.py:165
  43.8 8.6 %collective-permute-start.15 = (f32[128,384]{1,0:T(8,128)S(1)}, f32[128,384]{1,0:T(8,128)S(1)}, u32[]{:S(2)}, u32[]{:S(2)}) collective-permute-start(f32[128,384]{1,0:T(8,128)S(1)} %get-tuple-element.262), channel_id=1, source_target_pairs={{0,16},{8,24},{16,0},{24,8},{1,17},{9,25},{17,1},{25,9},{2,18},{10... | collective-permute-start | bytes 589832 | tf_op jit(solution)/shard_map/ppermute | solution.py:165
  56.1 8.5 %collective-permute-start.19 = (f32[40,384]{1,0:T(8,128)S(1)}, f32[40,384]{1,0:T(8,128)S(1)}, u32[]{:S(2)}, u32[]{:S(2)}) collective-permute-start(f32[40,384]{1,0:T(8,128)S(1)} %get-tuple-element.277), channel_id=1, source_target_pairs={{0,4},{1,5},{2,6},{3,7},{4,0},{5,1},{6,2},{7,3},{8,12},{9,13},{10,... | collective-permute-start | bytes 184328 | tf_op jit(solution)/shard_map/ppermute | solution.py:175
  83.3 13.0 %collective-permute-start.29 = (f32[160,384]{1,0:T(8,128)S(1)}, f32[160,384]{1,0:T(8,128)S(1)}, u32[]{:S(2)}, u32[]{:S(2)}) collective-permute-start(f32[160,384]{1,0:T(8,128)S(1)} %get-tuple-element.254), channel_id=1, source_target_pairs={{0,8},{8,0},{16,24},{24,16},{1,9},{9,1},{17,25},{25,17},{2,10},{10... | collective-permute-start | bytes 737288 | tf_op jit(solution)/shard_map/ppermute | solution.py:165
  83.7 14.0 %collective-permute-start.30 = (f32[160,384]{1,0:T(8,128)S(1)}, f32[160,384]{1,0:T(8,128)S(1)}, u32[]{:S(2)}, u32[]{:S(2)}) collective-permute-start(f32[160,384]{1,0:T(8,128)S(1)} %get-tuple-element.253), channel_id=1, source_target_pairs={{0,16},{8,24},{16,0},{24,8},{1,17},{9,25},{17,1},{25,9},{2,18},{10... | collective-permute-start | bytes 737288 | tf_op jit(solution)/shard_map/ppermute | solution.py:165
  85.4 12.3 %collective-permute-start.31 = (f32[160,384]{1,0:T(8,128)S(1)}, f32[160,384]{1,0:T(8,128)S(1)}, u32[]{:S(2)}, u32[]{:S(2)}) collective-permute-start(f32[160,384]{1,0:T(8,128)S(1)} %get-tuple-element.252), channel_id=1, source_target_pairs={{0,24},{8,16},{16,8},{24,0},{1,25},{9,17},{17,9},{25,1},{2,26},{10... | collective-permute-start | bytes 737288 | tf_op jit(solution)/shard_map/ppermute | solution.py:165
  94.6 9.6 %collective-permute-start.24 = (f32[160,384]{1,0:T(8,128)S(1)}, f32[160,384]{1,0:T(8,128)S(1)}, u32[]{:S(2)}, u32[]{:S(2)}) collective-permute-start(f32[160,384]{1,0:T(8,128)S(1)} %get-tuple-element.256), channel_id=1, source_target_pairs={{0,16},{8,24},{16,0},{24,8},{1,17},{9,25},{17,1},{25,9},{2,18},{10... | collective-permute-start | bytes 737288 | tf_op jit(solution)/shard_map/ppermute | solution.py:165
  109.6 11.0 %collective-permute-start.36 = (f32[128,384]{1,0:T(8,128)S(1)}, f32[128,384]{1,0:T(8,128)S(1)}, u32[]{:S(2)}, u32[]{:S(2)}) collective-permute-start(f32[128,384]{1,0:T(8,128)S(1)} %shard_map.307.refs_1_), channel_id=1, source_target_pairs={{0,8},{8,0},{16,24},{24,16},{1,9},{9,1},{17,25},{25,17},{2,10},{10... | collective-permute-start | bytes 589832 | tf_op jit(solution)/shard_map/ppermute | solution.py:165
  110.8 10.9 %collective-permute-start.37 = (f32[128,384]{1,0:T(8,128)S(1)}, f32[128,384]{1,0:T(8,128)S(1)}, u32[]{:S(2)}, u32[]{:S(2)}) collective-permute-start(f32[128,384]{1,0:T(8,128)S(1)} %shard_map.307.refs_1_), channel_id=1, source_target_pairs={{0,16},{8,24},{16,0},{24,8},{1,17},{9,25},{17,1},{25,9},{2,18},{10... | collective-permute-start | bytes 589832 | tf_op jit(solution)/shard_map/ppermute | solution.py:165
  111.7 10.0 %collective-permute-start.38 = (f32[128,384]{1,0:T(8,128)S(1)}, f32[128,384]{1,0:T(8,128)S(1)}, u32[]{:S(2)}, u32[]{:S(2)}) collective-permute-start(f32[128,384]{1,0:T(8,128)S(1)} %shard_map.307.refs_1_), channel_id=1, source_target_pairs={{0,24},{8,16},{16,8},{24,0},{1,25},{9,17},{17,9},{25,1},{2,26},{10... | collective-permute-start | bytes 589832 | tf_op jit(solution)/shard_map/ppermute | solution.py:165
  136.4 9.2 %collective-permute-start.48 = (f32[2,96,384]{2,1,0:T(8,128)S(1)}, f32[2,96,384]{2,1,0:T(8,128)S(1)}, u32[]{:S(2)}, u32[]{:S(2)}) collective-permute-start(f32[2,96,384]{2,1,0:T(8,128)S(1)} %get-tuple-element.206.refs_26_), channel_id=1, source_target_pairs={{0,2},{1,3},{2,0},{3,1},{4,6},{5,7},{6,4},{7,5},{8,10},{9,11},{10,... | collective-permute-start | bytes 884744 | tf_op jit(solution)/shard_map/ppermute | solution.py:175
  143.5 10.6 %collective-permute-start.47 = (f32[2,96,384]{2,1,0:T(8,128)S(1)}, f32[2,96,384]{2,1,0:T(8,128)S(1)}, u32[]{:S(2)}, u32[]{:S(2)}) collective-permute-start(f32[2,96,384]{2,1,0:T(8,128)S(1)} %get-tuple-element.205.refs_27_), channel_id=1, source_target_pairs={{0,2},{1,3},{2,0},{3,1},{4,6},{5,7},{6,4},{7,5},{8,10},{9,11},{10,... | collective-permute-start | bytes 884744 | tf_op jit(solution)/shard_map/ppermute | solution.py:175
  145.6 8.5 %collective-permute-start.49 = (f32[1,96,384]{2,1,0:T(8,128)S(1)}, f32[1,96,384]{2,1,0:T(8,128)S(1)}, u32[]{:S(2)}, u32[]{:S(2)}) collective-permute-start(f32[1,96,384]{2,1,0:T(8,128)S(1)} %slice_add_fusion.11), channel_id=1, source_target_pairs={{0,4},{1,5},{2,6},{3,7},{4,0},{5,1},{6,2},{7,3},{8,12},{9,13},{10,... | collective-permute-start | bytes 442376 | tf_op jit(solution)/shard_map/ppermute | solution.py:175
  157.0 16.8 %collective-permute-start.62 = (f32[1,192,384]{2,1,0:T(8,128)S(1)}, f32[1,192,384]{2,1,0:T(8,128)S(1)}, u32[]{:S(2)}, u32[]{:S(2)}) collective-permute-start(f32[1,192,384]{2,1,0:T(8,128)S(1)} %pad_maximum_fusion.8), channel_id=1, source_target_pairs={{0,4},{1,5},{2,6},{3,7},{4,0},{5,1},{6,2},{7,3},{8,12},{9,13},{10,... | collective-permute-start | bytes 884744 | tf_op jit(solution)/shard_map/ppermute | solution.py:175
  161.7 12.1 %collective-permute-start.51 = (f32[136,384]{1,0:T(8,128)S(1)}, f32[136,384]{1,0:T(8,128)S(1)}, u32[]{:S(2)}, u32[]{:S(2)}) collective-permute-start(f32[136,384]{1,0:T(8,128)S(1)} %get-tuple-element.258), channel_id=1, source_target_pairs={{0,8},{8,0},{16,24},{24,16},{1,9},{9,1},{17,25},{25,17},{2,10},{10... | collective-permute-start | bytes 626696 | tf_op jit(solution)/shard_map/ppermute | solution.py:165
  162.6 11.5 %collective-permute-start.52 = (f32[136,384]{1,0:T(8,128)S(1)}, f32[136,384]{1,0:T(8,128)S(1)}, u32[]{:S(2)}, u32[]{:S(2)}) collective-permute-start(f32[136,384]{1,0:T(8,128)S(1)} %get-tuple-element.260), channel_id=1, source_target_pairs={{0,16},{8,24},{16,0},{24,8},{1,17},{9,25},{17,1},{25,9},{2,18},{10... | collective-permute-start | bytes 626696 | tf_op jit(solution)/shard_map/ppermute | solution.py:165
  163.9 15.8 %collective-permute-start.61 = (f32[2,120,384]{2,1,0:T(8,128)S(1)}, f32[2,120,384]{2,1,0:T(8,128)S(1)}, u32[]{:S(2)}, u32[]{:S(2)}) collective-permute-start(f32[2,120,384]{2,1,0:T(8,128)S(1)} %get-tuple-element.249), channel_id=1, source_target_pairs={{0,2},{1,3},{2,0},{3,1},{4,6},{5,7},{6,4},{7,5},{8,10},{9,11},{10,... | collective-permute-start | bytes 1105928 | tf_op jit(solution)/shard_map/ppermute | solution.py:175
  165.3 8.8 %collective-permute-start.53 = (f32[136,384]{1,0:T(8,128)S(1)}, f32[136,384]{1,0:T(8,128)S(1)}, u32[]{:S(2)}, u32[]{:S(2)}) collective-permute-start(f32[136,384]{1,0:T(8,128)S(1)} %get-tuple-element.259), channel_id=1, source_target_pairs={{0,24},{8,16},{16,8},{24,0},{1,25},{9,17},{17,9},{25,1},{2,26},{10... | collective-permute-start | bytes 626696 | tf_op jit(solution)/shard_map/ppermute | solution.py:165
  179.7 17.9 %collective-permute-start.64 = (f32[2,96,384]{2,1,0:T(8,128)S(1)}, f32[2,96,384]{2,1,0:T(8,128)S(1)}, u32[]{:S(2)}, u32[]{:S(2)}) collective-permute-start(f32[2,96,384]{2,1,0:T(8,128)S(1)} %pad_maximum_fusion.9), channel_id=1, source_target_pairs={{0,2},{1,3},{2,0},{3,1},{4,6},{5,7},{6,4},{7,5},{8,10},{9,11},{10,... | collective-permute-start | bytes 884744 | tf_op jit(solution)/shard_map/ppermute | solution.py:175
  179.9 17.5 %collective-permute-start.63 = (f32[1,216,384]{2,1,0:T(8,128)S(1)}, f32[1,216,384]{2,1,0:T(8,128)S(1)}, u32[]{:S(2)}, u32[]{:S(2)}) collective-permute-start(f32[1,216,384]{2,1,0:T(8,128)S(1)} %pad_maximum_fusion.7), channel_id=1, source_target_pairs={{0,4},{1,5},{2,6},{3,7},{4,0},{5,1},{6,2},{7,3},{8,12},{9,13},{10,... | collective-permute-start | bytes 995336 | tf_op jit(solution)/shard_map/ppermute | solution.py:175
  183.3 10.4 %collective-permute-start.55 = (f32[136,384]{1,0:T(8,128)S(1)}, f32[136,384]{1,0:T(8,128)S(1)}, u32[]{:S(2)}, u32[]{:S(2)}) collective-permute-start(f32[136,384]{1,0:T(8,128)S(1)} %add_add_fusion.refs_1_), channel_id=1, source_target_pairs={{0,16},{8,24},{16,0},{24,8},{1,17},{9,25},{17,1},{25,9},{2,18},{10... | collective-permute-start | bytes 626696 | tf_op jit(solution)/shard_map/ppermute | solution.py:165
  184.2 9.6 %collective-permute-start.56 = (f32[136,384]{1,0:T(8,128)S(1)}, f32[136,384]{1,0:T(8,128)S(1)}, u32[]{:S(2)}, u32[]{:S(2)}) collective-permute-start(f32[136,384]{1,0:T(8,128)S(1)} %add_add_fusion.refs_1_), channel_id=1, source_target_pairs={{0,24},{8,16},{16,8},{24,0},{1,25},{9,17},{17,9},{25,1},{2,26},{10... | collective-permute-start | bytes 626696 | tf_op jit(solution)/shard_map/ppermute | solution.py:165
  197.7 14.8 %collective-permute-start.67 = (f32[2,96,384]{2,1,0:T(8,128)S(1)}, f32[2,96,384]{2,1,0:T(8,128)S(1)}, u32[]{:S(2)}, u32[]{:S(2)}) collective-permute-start(f32[2,96,384]{2,1,0:T(8,128)S(1)} %pad_maximum_fusion.10), channel_id=1, source_target_pairs={{0,2},{1,3},{2,0},{3,1},{4,6},{5,7},{6,4},{7,5},{8,10},{9,11},{10,... | collective-permute-start | bytes 884744 | tf_op jit(solution)/shard_map/ppermute | solution.py:175
  198.4 11.6 %collective-permute-start.66 = (f32[1,128,384]{2,1,0:T(8,128)S(1)}, f32[1,128,384]{2,1,0:T(8,128)S(1)}, u32[]{:S(2)}, u32[]{:S(2)}) collective-permute-start(f32[1,128,384]{2,1,0:T(8,128)S(1)} %pad_maximum_fusion.16), channel_id=1, source_target_pairs={{0,4},{1,5},{2,6},{3,7},{4,0},{5,1},{6,2},{7,3},{8,12},{9,13},{10,... | collective-permute-start | bytes 589832 | tf_op jit(solution)/shard_map/ppermute | solution.py:175
  200.6 9.5 %collective-permute-start.57 = (f32[128,384]{1,0:T(8,128)S(1)}, f32[128,384]{1,0:T(8,128)S(1)}, u32[]{:S(2)}, u32[]{:S(2)}) collective-permute-start(f32[128,384]{1,0:T(8,128)S(1)} %shard_map.313.refs_1_), channel_id=1, source_target_pairs={{0,8},{8,0},{16,24},{24,16},{1,9},{9,1},{17,25},{25,17},{2,10},{10... | collective-permute-start | bytes 589832 | tf_op jit(solution)/shard_map/ppermute | solution.py:165
  201.9 10.6 %collective-permute-start.58 = (f32[128,384]{1,0:T(8,128)S(1)}, f32[128,384]{1,0:T(8,128)S(1)}, u32[]{:S(2)}, u32[]{:S(2)}) collective-permute-start(f32[128,384]{1,0:T(8,128)S(1)} %shard_map.313.refs_1_), channel_id=1, source_target_pairs={{0,16},{8,24},{16,0},{24,8},{1,17},{9,25},{17,1},{25,9},{2,18},{10... | collective-permute-start | bytes 589832 | tf_op jit(solution)/shard_map/ppermute | solution.py:165
  202.6 9.9 %collective-permute-start.59 = (f32[128,384]{1,0:T(8,128)S(1)}, f32[128,384]{1,0:T(8,128)S(1)}, u32[]{:S(2)}, u32[]{:S(2)}) collective-permute-start(f32[128,384]{1,0:T(8,128)S(1)} %shard_map.313.refs_1_), channel_id=1, source_target_pairs={{0,24},{8,16},{16,8},{24,0},{1,25},{9,17},{17,9},{25,1},{2,26},{10... | collective-permute-start | bytes 589832 | tf_op jit(solution)/shard_map/ppermute | solution.py:165
  212.6 11.5 %collective-permute-start.68 = (f32[4,192,384]{2,1,0:T(8,128)S(1)}, f32[4,192,384]{2,1,0:T(8,128)S(1)}, u32[]{:S(2)}, u32[]{:S(2)}) collective-permute-start(f32[4,192,384]{2,1,0:T(8,128)S(1)} %maximum_maximum_fusion), channel_id=1, source_target_pairs={{0,1},{1,0},{2,3},{3,2},{4,5},{5,4},{6,7},{7,6},{8,9},{9,8},{10,11... | collective-permute-start | bytes 3538952 | tf_op jit(solution)/shard_map/ppermute | solution.py:170
  212.7 11.3 %collective-permute-start.69 = (f32[1,248,384]{2,1,0:T(8,128)S(1)}, f32[1,248,384]{2,1,0:T(8,128)S(1)}, u32[]{:S(2)}, u32[]{:S(2)}) collective-permute-start(f32[1,248,384]{2,1,0:T(8,128)S(1)} %pad_maximum_fusion.5), channel_id=1, source_target_pairs={{0,2},{1,3},{2,0},{3,1},{4,6},{5,7},{6,4},{7,5},{8,10},{9,11},{10,... | collective-permute-start | bytes 1142792 | tf_op jit(solution)/shard_map/ppermute | solution.py:175
  (53 other events, 375.6 us)
where the time goes:
time: 233 us; the launch traced here: 230 us
  starting transfers between devices  82.1 us (35%)
  waiting for transfers between devices  66.9 us (29%)
  Pallas kernels  64 us (27%)
  blocking collectives  12.9 us (6%)
    pallas_call x24, Pallas kernels, call(): pl.pallas_call(run, out_shape=outs, in_specs=[pl.BlockSpec(memory_space=p...  64 us
    ppermute x28, waiting for transfers between devices, chip_swap(): return lax.ppermute(value, 'wide', [(i, i ^ 2 * key) for i in range(count)])  41.5 us
    ppermute x28, starting transfers between devices, chip_swap(): return lax.ppermute(value, 'wide', [(i, i ^ 2 * key) for i in range(count)])  38.6 us
    ppermute x31, starting transfers between devices, narrow_swap(): return lax.ppermute(value, 'narrow', [(i, i ^ key) for i in range(4)])  38.3 us
    ppermute x31, waiting for transfers between devices, narrow_swap(): return lax.ppermute(value, 'narrow', [(i, i ^ key) for i in range(4)])  22.8 us
    all_gather x1, blocking collectives, local(): hidden_parts = lax.all_gather(hold(hidden_blocks, raw), 'narrow')  12.9 us
  transfers between devices with their start and end apart: 71, of which 31 were waited for; matrix products, arithmetic and copies ran while one was open for 1% of the time, Pallas kernels for 18%

commit v1 on v0

--- a/solution.py
+++ b/solution.py
@@ -333,15 +333,14 @@
     gate_in[...] = product(parts, (gate_high[...], gate_low[...]))
 
 
-def start_kernel(capacity, ids, segments_far, expert_ids_far, tokens_far, cotangent_far, weight_far,
+def start_kernel(capacity, ids, segments_far, expert_ids_far, cotangent_far, weight_far,
                  marks, slots_own, slots_other, rows_own, rows_other,
-                 rows_slice, cot_slice, own, other, conv_high, conv_low, gate_high, gate_low,
-                 segments, expert_ids, tokens, cotangent, weight, rows, held, branch,
+                 cot_slice, own, other, conv_high, conv_low, gate_high, gate_low,
+                 segments, expert_ids, cotangent, weight, rows, held, branch,
                  sems):
     pairs = (
         (segments_far, segments),
         (expert_ids_far, expert_ids),
-        (tokens_far, tokens),
         (cotangent_far, cotangent),
         (weight_far, weight),
     )
@@ -355,40 +354,38 @@
     route_kernel(capacity, ids, segments, expert_ids, marks, slots_own, slots_other,
                  rows_own, rows_other)
     copies[2].wait()
+    interleave_from(cotangent, held, rows)
+    own_slice(ids[0], rows, cot_slice)
+    send_slots(ids[2], cot_slice[...], slots_own[...], slots_other[...], own, other)
     copies[3].wait()
-    slices_kernel(ids, tokens, cotangent, slots_own, slots_other, rows_slice, cot_slice, own, other,
-                  rows, held)
-    copies[4].wait()
     for k, (high, low) in enumerate(((conv_high, conv_low), (gate_high, gate_low))):
         branch[k] = weight[:, k, :]
         high[...], low[...] = two_parts(branch[k])
 
 
-def slices_kernel(ids, tokens, cotangent, slots_own, slots_other,
-                  rows_slice, cot_slice, own, other, rows, held):
-    me, core = ids[0], ids[2]
-    half, part = tokens.shape[0] // 2, tokens.shape[1] // 4
-    for source, out in ((tokens, rows_slice), (cotangent, cot_slice)):
-        interleave_from(source, held, rows)
-        for j in range(4):
-            @pl.when(me == j)
-            def _():
-                out[:, :part] = rows[:half, part * j : part * (j + 1)]
-                out[:, part:] = rows[half:, part * j : part * (j + 1)]
-    send_slots(core, cot_slice[...], slots_own[...], slots_other[...], own, other)
+def own_slice(me, rows, out):
+    half, part = rows.shape[0] // 2, rows.shape[1] // 4
+    for j in range(4):
+        @pl.when(me == j)
+        def _():
+            out[:, :part] = rows[:half, part * j : part * (j + 1)]
+            out[:, part:] = rows[half:, part * j : part * (j + 1)]
+
+
+def own_slice_kernel(ids, rows, out):
+    own_slice(ids[0], rows, out)
 
 
 def send_slots(core, packed, slots_own, slots_other, own, other):
     half = packed.shape[1] // 2
-    lane = lax.broadcasted_iota(jnp.int32, packed.shape, 1)
-    left = jnp.where(lane < half, packed, 0.0)
-    right = jnp.where(lane < half, 0.0, packed)
-    second = core == 1
-    top = jnp.where(second, pltpu.roll(left, half, 1), left)
-    bottom = jnp.where(second, right, pltpu.roll(right, half, 1))
-    placed = jnp.concatenate([top, bottom])
-    own[...] = select_rows(slots_own, placed)
-    other[...] = select_rows(slots_other, placed)
+    rows = jnp.concatenate([packed[:, :half], packed[:, half:]])
+    for slots, out in ((slots_own, own), (slots_other, other)):
+        sent = select_rows(slots, rows)
+        for side in range(2):
+            @pl.when(core == side)
+            def _():
+                out[:, side * half : (side + 1) * half] = sent
+                out[:, (1 - side) * half : (2 - side) * half] = jnp.zeros_like(sent)
 
 
 def conv_kernel(ids, halo, gain, conv_high, conv_low, conv_in, marks, conv_weight, conv_bias,
@@ -677,16 +674,14 @@
     second = ids[2] == 1
 
     def mine(rows):
-        return jnp.where(second, pltpu.roll(rows, half, 1), rows)
+        return jnp.where(second, rows[:, half:], rows[:, :half])
 
     total = select_rows(rows_own[...], mine(own[...])) + select_rows(
         rows_other[...], mine(other[...])
     )
     count = base.shape[0]
-    lane = lax.broadcasted_iota(jnp.int32, base.shape, 1)
-    out[...] = base[...] + jnp.where(
-        lane < half, total[:count], pltpu.roll(total[count:], half, 1)
-    )
+    out[:, :half] = base[:, :half] + total[:count]
+    out[:, half:] = base[:, half:] + total[count:]
 
 
 def whole_kernel(ids, p0, p1, p2, p3, out, held, whole, tiles):
@@ -1048,21 +1043,20 @@
 
     halo_rows = wide_shift(tokens[length - SEGMENTS :], 1)
 
-    (marks, slots_own, slots_other, rows_own, rows_other, rows_slice, cot_slice, cot_own,
-     cot_other, conv_high, conv_low, gate_high, gate_low) = call(
+    (marks, slots_own, slots_other, rows_own, rows_other, cot_slice, cot_own, cot_other,
+     conv_high, conv_low, gate_high, gate_low) = call(
         functools.partial(start_kernel, capacity),
         [shape_of(length, SEGMENTS)]
         + [shape_of(slots, length, dtype=bf16)] * 2
         + [shape_of(length, slots, dtype=bf16)] * 2
-        + [packed, packed, packed_slots, packed_slots]
+        + [packed, packed_slots, packed_slots]
         + [shape_of(width, channels, dtype=bf16)] * 4,
-        ids, segments.reshape(-1, LANES), expert_ids.reshape(1, length), tokens, cotangent,
-        in_weight,
+        ids, segments.reshape(-1, LANES), expert_ids.reshape(1, length), cotangent, in_weight,
         scratch=[pltpu.VMEM((segments.shape[0] // LANES, LANES), jnp.int32),
-                 pltpu.VMEM((1, length), jnp.int32)] + [vmem(length, width)] * 2
+                 pltpu.VMEM((1, length), jnp.int32)] + [vmem(length, width)]
         + [vmem(width, 2, channels), vmem(length, width), tiled, vmem(2, width, channels),
-           pltpu.SemaphoreType.DMA((5,))],
-        far_in=[0, 1, 2, 3, 4],
+           pltpu.SemaphoreType.DMA((4,))],
+        far_in=[0, 1, 2, 3],
     )
     cot_pair = cot_own + core_swap(cot_other)
     rows, normed, conv_in, gate_in = call(
@@ -1112,6 +1106,7 @@
         out_place=[3],
     )
     mixer_slices = hold(mixer_slices, cot_one, cot_two)
+    (rows_slice,) = call(own_slice_kernel, [packed], ids, rows, after=[mixer_slices])
     expert_rows, square = shape_of(2 * slots, width), (expert_in.shape[1], expert_in.shape[2])
     hidden_units = square[1]
     hidden_slice, hidden_own, hidden_other = call(

time: 233 us -> 242 us (1.039)
  Pallas kernels: 64 us -> 73.4 us
    pallas_call x24 -> x25, Pallas kernels: 64 us -> 73.4 us  [call(): pl.pallas_call(run, out_shape=outs, in_specs=[pl.BlockSpec(memory_space=p...]
  transfers between devices with their start and end apart: 71 -> 71, of which waited for: 31 -> 31; matrix products, arithmetic and copies ran while one was open for 1% -> 0% of each run, Pallas kernels for 18% -> 18%
where the time goes in v1:
time: 242 us; the launch traced here: 238 us
  starting transfers between devices  81.4 us (34%)
  Pallas kernels  73.4 us (30%)
  waiting for transfers between devices  66.7 us (28%)
  blocking collectives  12.5 us (5%)
    pallas_call x25, Pallas kernels, call(): pl.pallas_call(run, out_shape=outs, in_specs=[pl.BlockSpec(memory_space=p...  73.4 us
    ppermute x28, waiting for transfers between devices, chip_swap(): return lax.ppermute(value, 'wide', [(i, i ^ 2 * key) for i in range(count)])  41 us
    ppermute x31, starting transfers between devices, narrow_swap(): return lax.ppermute(value, 'narrow', [(i, i ^ key) for i in range(4)])  38.1 us
    ppermute x28, starting transfers between devices, chip_swap(): return lax.ppermute(value, 'wide', [(i, i ^ 2 * key) for i in range(count)])  38 us
    ppermute x31, waiting for transfers between devices, narrow_swap(): return lax.ppermute(value, 'narrow', [(i, i ^ key) for i in range(4)])  22.6 us
    all_gather x1, blocking collectives, local(): hidden_parts = lax.all_gather(hold(hidden_blocks, raw), 'narrow')  12.5 us
  transfers between devices with their start and end apart: 71, of which 31 were waited for; matrix products, arithmetic and copies ran while one was open for 0% of the time, Pallas kernels for 18%

profile of v1, /device:TPU:0, one launch (start us, length us, event | category | flops | bytes accessed | tf_op | source)
XLA Modules:
  0.0 237.8 jit_solution(3559413583853822827)
XLA Ops:
  0.7 3.7 %shard_map.297 = (f32[256,8]{1,0:T(8,128)S(1)}, bf16[160,256]{1,0:T(8,128)(2,1)S(1)}, bf16[160,256]{1,0:T(8,128)(2,1)S(1)}, bf16[256,160]{1,0:T(8,128)(2,1)S(1)}...) custom-call(s32[4]{0:T(128)S(1)} %pad_add_fusion.refs_0_, ...), custom_call_target="tpu_custom_call" | custom-call | flops 1 | bytes 1 | tf_op jit(solution)/shard_map/pallas_call | solution.py:46
  7.2 2.6 %shard_map.298 = (f32[256,768]{1,0:T(8,128)S(1)}, f32[256,768]{1,0:T(8,128)S(1)}, f32[256,384]{1,0:T(8,128)S(1)}, f32[256,384]{1,0:T(8,128)S(1)}) custom-call(s32[4]{0:T(128)S(1)} %pad_add_fusion.refs_0_, f32[256,768]{1,0:T(8,128)S(1)} %copy-done.3, f32[768]{0:T(1024)S(1)} %copy-done.6, bf16[768,384]{1,0:T(8,128)(2,1)S(1)} %get-tuple-element.129.refs_3_, ...), custom_call_target="tpu_custom_call" | custom-call | flops 1 | bytes 1 | tf_op jit(solution)/shard_map/pallas_call | solution.py:46
  11.3 2.8 %collective-permute-start.2 = (f32[80,256]{1,0:T(8,128)S(1)}, f32[80,256]{1,0:T(8,128)S(1)}, u32[]{:S(2)}, u32[]{:S(2)}) collective-permute-start(f32[80,256]{1,0:T(8,128)S(1)} %get-tuple-element.137.refs_1_), channel_id=1, source_target_pairs={{0,8},{8,0},{16,24},{24,16},{1,9},{9,1},{17,25},{25,17},{2,10},{10... | collective-permute-start | bytes 245768 | tf_op jit(solution)/shard_map/ppermute | solution.py:165
  15.7 2.2 collective-permute-start.6
  17.9 2.6 %collective-permute-start.7 = (f32[40,384]{1,0:T(8,128)S(1)}, f32[40,384]{1,0:T(8,128)S(1)}, u32[]{:S(2)}, u32[]{:S(2)}) collective-permute-start(f32[40,384]{1,0:T(8,128)S(1)} %get-tuple-element.279), channel_id=1, source_target_pairs={{0,4},{1,5},{2,6},{3,7},{4,0},{5,1},{6,2},{7,3},{8,12},{9,13},{10,... | collective-permute-start | bytes 184328 | tf_op jit(solution)/shard_map/ppermute | solution.py:175
  21.6 2.6 %shard_map.300 = (f32[256,128]{1,0:T(8,128)S(1)}, f32[256,384]{1,0:T(8,128)S(1)}, f32[256,384]{1,0:T(8,128)S(1)}, f32[256,384]{1,0:T(8,128)S(1)}, f32[256,384]{1...) custom-call(s32[4]{0:T(128)S(1)} %pad_add_fusion.refs_0_, ...), custom_call_target="tpu_custom_call" | custom-call | flops 1 | bytes 1 | tf_op jit(solution)/shard_map/pallas_call | solution.py:46
  37.7 4.4 %shard_map.302 = (f32[256,384]{1,0:T(8,128)S(1)}, f32[256,384]{1,0:T(8,128)S(1)}, f32[4,128,384]{2,1,0:T(8,128)S(1)}, f32[4,33,4,8,384]{4,3,2,1,0:T(8,128)S(1)}) custom-call(s32[4]{0:T(128)S(1)} %pad_add_fusion.refs_0_, f32[256,384]{1,0:T(8,128)S(1)} %get-tuple-element.139.refs_1_.refs_9_, f32[256,384]{1,0:T(8,128)S(1)} %get-tuple-element.140.refs_2_, ...), custom_call_target="tpu_custom_call" | custom-call | flops 1 | bytes 1 | tf_op jit(solution)/shard_map/pallas_call | solution.py:46
  43.3 2.5 %collective-permute-start.16 = (f32[128,384]{1,0:T(8,128)S(1)}, f32[128,384]{1,0:T(8,128)S(1)}, u32[]{:S(2)}, u32[]{:S(2)}) collective-permute-start(f32[128,384]{1,0:T(8,128)S(1)} %get-tuple-element.259), channel_id=1, source_target_pairs={{0,24},{8,16},{16,8},{24,0},{1,25},{9,17},{17,9},{25,1},{2,26},{10... | collective-permute-start | bytes 589832 | tf_op jit(solution)/shard_map/ppermute | solution.py:165
  46.4 2.7 %collective-permute-done.14.refs_2_ = f32[128,384]{1,0:T(8,128)S(1)} collective-permute-done((f32[128,384]{1,0:T(8,128)S(1)}, f32[128,384]{1,0:T(8,128)S(1)}, u32[]{:S(2)}, u32[]{:S(2)}) %collective-permute-start.14) | collective-permute-done | bytes 196640 | tf_op jit(solution)/shard_map/ppermute | solution.py:165
  49.1 2.4 collective-permute-done.15.refs_3_
  55.4 2.4 collective-permute-start.19
  59.8 2.8 %shard_map.305 = (f32[320,768]{1,0:T(8,128)S(1)}, f32[320,768]{1,0:T(8,128)S(1)}, bf16[768,768]{1,0:T(8,128)(2,1)S(1)}, bf16[768,768]{1,0:T(8,128)(2,1)S(1)}, bf...) custom-call(s32[4]{0:T(128)S(1)} %pad_add_fusion.refs_0_, f32[160,384]{1,0:T(8,128)S(1)} %pad_maximum_fusion.11.refs_4_.refs_1_, ...), custom_call_target="tpu_custom_call" | custom-call | flops 1 | bytes 1 | tf_op jit(solution)/shard_map/pallas_call | solution.py:46
  63.9 12.5 %all-gather = f32[640,384]{1,0:T(8,128)S(1)} all-gather(f32[160,384]{1,0:T(8,128)S(1)} %pad_maximum_fusion.12), channel_id=2, replica_groups=mesh['narrow'=4,'wide'=8] {'narrow'}, dimensions={0}, use_global_device_ids=true | all-gather | bytes 1228800 | tf_op jit(solution)/shard_map/all_gather | solution.py:1128
  76.4 5.8 %shard_map.306 = (f32[4,160,384]{2,1,0:T(8,128)S(1)}, f32[320,768]{1,0:T(8,128)S(1)}, f32[320,768]{1,0:T(8,128)S(1)}, f32[320,768]{1,0:T(8,128)S(1)}, f32[320,1]...) custom-call(s32[4]{0:T(128)S(1)} %pad_add_fusion.refs_0_, f32[4,160,384]{2,1,0:T(8,128)S(1)} %bitcast.58, ...), custom_call_target="tpu_custom_call" | custom-call | flops 1 | bytes 1 | tf_op jit(solution)/shard_map/pallas_call | solution.py:46
  85.9 7.3 %shard_map.307 = (f32[4,160,384]{2,1,0:T(8,128)S(1)}, f32[768,768]{1,0:T(8,128)}, f32[768,768]{1,0:T(8,128)}, f32[8,768]{1,0:T(8,128)S(1)}) custom-call(s32[4]{0:T(128)S(1)} %pad_add_fusion.refs_0_, f32[320,768]{1,0:T(8,128)S(1)} %get-tuple-element.163.refs_1_, f32[320,768]{1,0:T(8,128)S(1)} %get-tuple-element.164.refs_2_, ...), custom_call_target="tpu_custom_call" | custom-call | flops 1 | bytes 1 | tf_op jit(solution)/shard_map/pallas_call | solution.py:46
  103.3 2.4 %collective-permute-done.34 = f32[40,384]{1,0:T(8,128)S(1)} collective-permute-done((f32[40,384]{1,0:T(8,128)S(1)}, f32[40,384]{1,0:T(8,128)S(1)}, u32[]{:S(2)}, u32[]{:S(2)}) %collective-permute-start.34) | collective-permute-done | bytes 61472 | tf_op jit(solution)/shard_map/ppermute | solution.py:175
  115.0 4.4 %collective-permute-done.27 = f32[40,384]{1,0:T(8,128)S(1)} collective-permute-done((f32[40,384]{1,0:T(8,128)S(1)}, f32[40,384]{1,0:T(8,128)S(1)}, u32[]{:S(2)}, u32[]{:S(2)}) %collective-permute-start.27) | collective-permute-done | bytes 61472 | tf_op jit(solution)/shard_map/ppermute | solution.py:175
  120.6 12.6 %shard_map.309 = (f32[256,768]{1,0:T(8,128)S(1)}, f32[256,384]{1,0:T(8,128)S(1)}, f32[256,384]{1,0:T(8,128)S(1)}, f32[1,384]{1,0:T(1,128)S(1)}, f32[2,16,8,384]{3,2,1,0:T(8,128)S(1)}, /*index=5*/f32[16,384]{1,0:T(8,128)S(1)}) custom-call(s32[4]{0:T(128)S(1)} %pad_add_fusion.refs_0_, f32[128,384]{1,0:T(8,128)S(1)} %shard_map.308.refs_1_, ...), custom_call_target="tpu_custom_call" | custom-call | flops 1 | bytes 1 | tf_op jit(solution)/shard_map/pallas_call | solution.py:46
  142.0 2.6 %collective-permute-done.42.refs_25_ = f32[16,384]{1,0:T(8,128)S(1)} collective-permute-done((f32[16,384]{1,0:T(8,128)S(1)}, f32[16,384]{1,0:T(8,128)S(1)}, u32[]{:S(2)}, u32[]{:S(2)}) %collective-permute-start.42) | collective-permute-done | bytes 24608 | tf_op jit(solution)/shard_map/ppermute | solution.py:175
  144.7 7.1 %shard_map.312 = (f32[112,256]{1,0:T(8,128)S(1)}, f32[256,384]{1,0:T(8,128)S(1)}, f32[256,384]{1,0:T(8,128)S(1)}, f32[16,384]{1,0:T(8,128)S(1)}, f32[1,384]{1,0:T(1,128)S(1)}) custom-call(s32[4]{0:T(128)S(1)} %pad_add_fusion.refs_0_, f32[256,384]{1,0:T(8,128)S(1)} %get-tuple-element.139.refs_1_.refs_9_, f32[256,384]{1,0:T(8,128)S(1)} %get-tuple-element.140.refs_2_, ...), custom_call_target="tpu_custom_call" | custom-call | flops 1 | bytes 1 | tf_op jit(solution)/shard_map/pallas_call | solution.py:46
  162.3 2.7 %shard_map.313 = (f32[4,120,384]{2,1,0:T(8,128)S(1)}, f32[4,120,384]{2,1,0:T(8,128)S(1)}, f32[256,384]{1,0:T(8,128)S(1)}, f32[8,384]{1,0:T(8,128)S(1)}) custom-call(s32[4]{0:T(128)S(1)} %pad_add_fusion.refs_0_, f32[112,256]{1,0:T(8,128)S(1)} %get-tuple-element.195.refs_1_.refs_4_, f32[112,256]{1,0:T(8,128)S(1)} %collective-permute-done.44.refs_2_, ...), custom_call_target="tpu_custom_call" | custom-call | flops 1 | bytes 1 | tf_op jit(solution)/shard_map/pallas_call | solution.py:46
  165.2 2.7 %collective-permute-start.62 = (f32[1,192,384]{2,1,0:T(8,128)S(1)}, f32[1,192,384]{2,1,0:T(8,128)S(1)}, u32[]{:S(2)}, u32[]{:S(2)}) collective-permute-start(f32[1,192,384]{2,1,0:T(8,128)S(1)} %pad_maximum_fusion.8), channel_id=1, source_target_pairs={{0,4},{1,5},{2,6},{3,7},{4,0},{5,1},{6,2},{7,3},{8,12},{9,13},{10,... | collective-permute-start | bytes 884744 | tf_op jit(solution)/shard_map/ppermute | solution.py:175
  176.1 5.9 %collective-permute-done.62 = f32[1,192,384]{2,1,0:T(8,128)S(1)} collective-permute-done((f32[1,192,384]{2,1,0:T(8,128)S(1)}, f32[1,192,384]{2,1,0:T(8,128)S(1)}, u32[]{:S(2)}, u32[]{:S(2)}) %collective-permute-start.62) | collective-permute-done | bytes 294944 | tf_op jit(solution)/shard_map/ppermute | solution.py:175
  182.3 5.6 %collective-permute-done.61 = f32[2,120,384]{2,1,0:T(8,128)S(1)} collective-permute-done((f32[2,120,384]{2,1,0:T(8,128)S(1)}, f32[2,120,384]{2,1,0:T(8,128)S(1)}, u32[]{:S(2)}, u32[]{:S(2)}) %collective-permute-start.61) | collective-permute-done | bytes 368672 | tf_op jit(solution)/shard_map/ppermute | solution.py:175
  193.9 4.6 %collective-permute-done.54.refs_2_ = f32[136,384]{1,0:T(8,128)S(1)} collective-permute-done((f32[136,384]{1,0:T(8,128)S(1)}, f32[136,384]{1,0:T(8,128)S(1)}, u32[]{:S(2)}, u32[]{:S(2)}) %collective-permute-start.54) | collective-permute-done | bytes 208928 | tf_op jit(solution)/shard_map/ppermute | solution.py:165
  198.5 3.1 %collective-permute-done.55.refs_3_ = f32[136,384]{1,0:T(8,128)S(1)} collective-permute-done((f32[136,384]{1,0:T(8,128)S(1)}, f32[136,384]{1,0:T(8,128)S(1)}, u32[]{:S(2)}, u32[]{:S(2)}) %collective-permute-start.55) | collective-permute-done | bytes 208928 | tf_op jit(solution)/shard_map/ppermute | solution.py:165
  206.3 2.6 %collective-permute-start.66 = (f32[1,128,384]{2,1,0:T(8,128)S(1)}, f32[1,128,384]{2,1,0:T(8,128)S(1)}, u32[]{:S(2)}, u32[]{:S(2)}) collective-permute-start(f32[1,128,384]{2,1,0:T(8,128)S(1)} %pad_maximum_fusion.16), channel_id=1, source_target_pairs={{0,4},{1,5},{2,6},{3,7},{4,0},{5,1},{6,2},{7,3},{8,12},{9,13},{10,... | collective-permute-start | bytes 589832 | tf_op jit(solution)/shard_map/ppermute | solution.py:175
  212.4 2.7 %shard_map.319 = f32[256,768]{1,0:T(8,128)} custom-call(s32[4]{0:T(128)S(1)} %pad_add_fusion.refs_0_, f32[136,384]{1,0:T(8,128)S(1)} %add_add_fusion.refs_1_, f32[136,384]{1,0:T(8,128)S(1)} %collective-permute-done.54.refs_2_, f32[136,384]{1,0:T(8,128)S(1)} %collective-permute-done.55.refs_3_, f32[136,384]{1,0:T(8,128)S(1)} %collective-permute-done.56.refs_4_, ...), custom_call_target="tpu_custom_call" | custom-call | flops 1 | bytes 1 | tf_op jit(solution)/shard_map/pallas_call | solution.py:46
  215.1 2.3 collective-permute-done.66
  217.4 3.2 %collective-permute-done.58.refs_3_ = f32[128,384]{1,0:T(8,128)S(1)} collective-permute-done((f32[128,384]{1,0:T(8,128)S(1)}, f32[128,384]{1,0:T(8,128)S(1)}, u32[]{:S(2)}, u32[]{:S(2)}) %collective-permute-start.58) | collective-permute-done | bytes 196640 | tf_op jit(solution)/shard_map/ppermute | solution.py:165
  225.0 7.3 %collective-permute-done.69 = f32[1,248,384]{2,1,0:T(8,128)S(1)} collective-permute-done((f32[1,248,384]{2,1,0:T(8,128)S(1)}, f32[1,248,384]{2,1,0:T(8,128)S(1)}, u32[]{:S(2)}, u32[]{:S(2)}) %collective-permute-start.69) | collective-permute-done | bytes 380960 | tf_op jit(solution)/shard_map/ppermute | solution.py:175
  235.0 2.5 %shard_map.321 = (f32[768,2,384]{2,1,0:T(2,128)}, f32[80,384]{1,0:T(8,128)}, f32[48,384]{1,0:T(8,128)}, f32[16,384]{1,0:T(8,128)}, f32[4,384]{1,0:T(4,128)}, /*i...) custom-call(s32[4]{0:T(128)S(1)} %pad_add_fusion.refs_0_, ...), custom_call_target="tpu_custom_call" | custom-call | flops 1 | bytes 1 | tf_op jit(solution)/shard_map/pallas_call | solution.py:46
  (217 shorter events, 102.5 us)
Async XLA Ops:
  11.3 9.2 %collective-permute-start.2 = (f32[80,256]{1,0:T(8,128)S(1)}, f32[80,256]{1,0:T(8,128)S(1)}, u32[]{:S(2)}, u32[]{:S(2)}) collective-permute-start(f32[80,256]{1,0:T(8,128)S(1)} %get-tuple-element.137.refs_1_), channel_id=1, source_target_pairs={{0,8},{8,0},{16,24},{24,16},{1,9},{9,1},{17,25},{25,17},{2,10},{10... | collective-permute-start | bytes 245768 | tf_op jit(solution)/shard_map/ppermute | solution.py:165
  15.7 8.6 %collective-permute-start.6 = (f32[40,384]{1,0:T(8,128)S(1)}, f32[40,384]{1,0:T(8,128)S(1)}, u32[]{:S(2)}, u32[]{:S(2)}) collective-permute-start(f32[40,384]{1,0:T(8,128)S(1)} %get-tuple-element.280), channel_id=1, source_target_pairs={{0,2},{1,3},{2,0},{3,1},{4,6},{5,7},{6,4},{7,5},{8,10},{9,11},{10,... | collective-permute-start | bytes 184328 | tf_op jit(solution)/shard_map/ppermute | solution.py:175
  27.2 14.9 %collective-permute-start.12 = (f32[160,384]{1,0:T(8,128)S(1)}, f32[160,384]{1,0:T(8,128)S(1)}, u32[]{:S(2)}, u32[]{:S(2)}) collective-permute-start(f32[160,384]{1,0:T(8,128)S(1)} %pad_maximum_fusion.11.refs_4_.refs_1_), channel_id=1, source_target_pairs={{0,8},{8,0},{16,24},{24,16},{1,9},{9,1},{17,25},{25,17},{2,10},{10... | collective-permute-start | bytes 737288 | tf_op jit(solution)/shard_map/ppermute | solution.py:165
  28.7 13.4 %collective-permute-start.13 = (f32[160,384]{1,0:T(8,128)S(1)}, f32[160,384]{1,0:T(8,128)S(1)}, u32[]{:S(2)}, u32[]{:S(2)}) collective-permute-start(f32[160,384]{1,0:T(8,128)S(1)} %pad_maximum_fusion.11.refs_4_.refs_1_), channel_id=1, source_target_pairs={{0,16},{8,24},{16,0},{24,8},{1,17},{9,25},{17,1},{25,9},{2,18},{10... | collective-permute-start | bytes 737288 | tf_op jit(solution)/shard_map/ppermute | solution.py:165
  42.8 8.6 %collective-permute-start.15 = (f32[128,384]{1,0:T(8,128)S(1)}, f32[128,384]{1,0:T(8,128)S(1)}, u32[]{:S(2)}, u32[]{:S(2)}) collective-permute-start(f32[128,384]{1,0:T(8,128)S(1)} %get-tuple-element.260), channel_id=1, source_target_pairs={{0,16},{8,24},{16,0},{24,8},{1,17},{9,25},{17,1},{25,9},{2,18},{10... | collective-permute-start | bytes 589832 | tf_op jit(solution)/shard_map/ppermute | solution.py:165
  55.4 8.5 %collective-permute-start.19 = (f32[40,384]{1,0:T(8,128)S(1)}, f32[40,384]{1,0:T(8,128)S(1)}, u32[]{:S(2)}, u32[]{:S(2)}) collective-permute-start(f32[40,384]{1,0:T(8,128)S(1)} %get-tuple-element.275), channel_id=1, source_target_pairs={{0,4},{1,5},{2,6},{3,7},{4,0},{5,1},{6,2},{7,3},{8,12},{9,13},{10,... | collective-permute-start | bytes 184328 | tf_op jit(solution)/shard_map/ppermute | solution.py:175
  82.3 13.0 %collective-permute-start.29 = (f32[160,384]{1,0:T(8,128)S(1)}, f32[160,384]{1,0:T(8,128)S(1)}, u32[]{:S(2)}, u32[]{:S(2)}) collective-permute-start(f32[160,384]{1,0:T(8,128)S(1)} %get-tuple-element.252), channel_id=1, source_target_pairs={{0,8},{8,0},{16,24},{24,16},{1,9},{9,1},{17,25},{25,17},{2,10},{10... | collective-permute-start | bytes 737288 | tf_op jit(solution)/shard_map/ppermute | solution.py:165
  82.7 14.0 %collective-permute-start.30 = (f32[160,384]{1,0:T(8,128)S(1)}, f32[160,384]{1,0:T(8,128)S(1)}, u32[]{:S(2)}, u32[]{:S(2)}) collective-permute-start(f32[160,384]{1,0:T(8,128)S(1)} %get-tuple-element.251), channel_id=1, source_target_pairs={{0,16},{8,24},{16,0},{24,8},{1,17},{9,25},{17,1},{25,9},{2,18},{10... | collective-permute-start | bytes 737288 | tf_op jit(solution)/shard_map/ppermute | solution.py:165
  84.4 12.3 %collective-permute-start.31 = (f32[160,384]{1,0:T(8,128)S(1)}, f32[160,384]{1,0:T(8,128)S(1)}, u32[]{:S(2)}, u32[]{:S(2)}) collective-permute-start(f32[160,384]{1,0:T(8,128)S(1)} %get-tuple-element.250), channel_id=1, source_target_pairs={{0,24},{8,16},{16,8},{24,0},{1,25},{9,17},{17,9},{25,1},{2,26},{10... | collective-permute-start | bytes 737288 | tf_op jit(solution)/shard_map/ppermute | solution.py:165
  93.6 9.6 %collective-permute-start.24 = (f32[160,384]{1,0:T(8,128)S(1)}, f32[160,384]{1,0:T(8,128)S(1)}, u32[]{:S(2)}, u32[]{:S(2)}) collective-permute-start(f32[160,384]{1,0:T(8,128)S(1)} %get-tuple-element.254), channel_id=1, source_target_pairs={{0,16},{8,24},{16,0},{24,8},{1,17},{9,25},{17,1},{25,9},{2,18},{10... | collective-permute-start | bytes 737288 | tf_op jit(solution)/shard_map/ppermute | solution.py:165
  108.4 11.0 %collective-permute-start.36 = (f32[128,384]{1,0:T(8,128)S(1)}, f32[128,384]{1,0:T(8,128)S(1)}, u32[]{:S(2)}, u32[]{:S(2)}) collective-permute-start(f32[128,384]{1,0:T(8,128)S(1)} %shard_map.308.refs_1_), channel_id=1, source_target_pairs={{0,8},{8,0},{16,24},{24,16},{1,9},{9,1},{17,25},{25,17},{2,10},{10... | collective-permute-start | bytes 589832 | tf_op jit(solution)/shard_map/ppermute | solution.py:165
  109.7 10.9 %collective-permute-start.37 = (f32[128,384]{1,0:T(8,128)S(1)}, f32[128,384]{1,0:T(8,128)S(1)}, u32[]{:S(2)}, u32[]{:S(2)}) collective-permute-start(f32[128,384]{1,0:T(8,128)S(1)} %shard_map.308.refs_1_), channel_id=1, source_target_pairs={{0,16},{8,24},{16,0},{24,8},{1,17},{9,25},{17,1},{25,9},{2,18},{10... | collective-permute-start | bytes 589832 | tf_op jit(solution)/shard_map/ppermute | solution.py:165
  110.5 10.1 %collective-permute-start.38 = (f32[128,384]{1,0:T(8,128)S(1)}, f32[128,384]{1,0:T(8,128)S(1)}, u32[]{:S(2)}, u32[]{:S(2)}) collective-permute-start(f32[128,384]{1,0:T(8,128)S(1)} %shard_map.308.refs_1_), channel_id=1, source_target_pairs={{0,24},{8,16},{16,8},{24,0},{1,25},{9,17},{17,9},{25,1},{2,26},{10... | collective-permute-start | bytes 589832 | tf_op jit(solution)/shard_map/ppermute | solution.py:165
  144.7 9.2 %collective-permute-start.48 = (f32[2,96,384]{2,1,0:T(8,128)S(1)}, f32[2,96,384]{2,1,0:T(8,128)S(1)}, u32[]{:S(2)}, u32[]{:S(2)}) collective-permute-start(f32[2,96,384]{2,1,0:T(8,128)S(1)} %get-tuple-element.205.refs_26_), channel_id=1, source_target_pairs={{0,2},{1,3},{2,0},{3,1},{4,6},{5,7},{6,4},{7,5},{8,10},{9,11},{10,... | collective-permute-start | bytes 884744 | tf_op jit(solution)/shard_map/ppermute | solution.py:175
  151.7 10.6 %collective-permute-start.47 = (f32[2,96,384]{2,1,0:T(8,128)S(1)}, f32[2,96,384]{2,1,0:T(8,128)S(1)}, u32[]{:S(2)}, u32[]{:S(2)}) collective-permute-start(f32[2,96,384]{2,1,0:T(8,128)S(1)} %get-tuple-element.204.refs_27_), channel_id=1, source_target_pairs={{0,2},{1,3},{2,0},{3,1},{4,6},{5,7},{6,4},{7,5},{8,10},{9,11},{10,... | collective-permute-start | bytes 884744 | tf_op jit(solution)/shard_map/ppermute | solution.py:175
  153.8 8.5 %collective-permute-start.49 = (f32[1,96,384]{2,1,0:T(8,128)S(1)}, f32[1,96,384]{2,1,0:T(8,128)S(1)}, u32[]{:S(2)}, u32[]{:S(2)}) collective-permute-start(f32[1,96,384]{2,1,0:T(8,128)S(1)} %slice_add_fusion.11), channel_id=1, source_target_pairs={{0,4},{1,5},{2,6},{3,7},{4,0},{5,1},{6,2},{7,3},{8,12},{9,13},{10,... | collective-permute-start | bytes 442376 | tf_op jit(solution)/shard_map/ppermute | solution.py:175
  165.2 16.8 %collective-permute-start.62 = (f32[1,192,384]{2,1,0:T(8,128)S(1)}, f32[1,192,384]{2,1,0:T(8,128)S(1)}, u32[]{:S(2)}, u32[]{:S(2)}) collective-permute-start(f32[1,192,384]{2,1,0:T(8,128)S(1)} %pad_maximum_fusion.8), channel_id=1, source_target_pairs={{0,4},{1,5},{2,6},{3,7},{4,0},{5,1},{6,2},{7,3},{8,12},{9,13},{10,... | collective-permute-start | bytes 884744 | tf_op jit(solution)/shard_map/ppermute | solution.py:175
  170.0 12.1 %collective-permute-start.51 = (f32[136,384]{1,0:T(8,128)S(1)}, f32[136,384]{1,0:T(8,128)S(1)}, u32[]{:S(2)}, u32[]{:S(2)}) collective-permute-start(f32[136,384]{1,0:T(8,128)S(1)} %get-tuple-element.256), channel_id=1, source_target_pairs={{0,8},{8,0},{16,24},{24,16},{1,9},{9,1},{17,25},{25,17},{2,10},{10... | collective-permute-start | bytes 626696 | tf_op jit(solution)/shard_map/ppermute | solution.py:165
  170.8 11.5 %collective-permute-start.52 = (f32[136,384]{1,0:T(8,128)S(1)}, f32[136,384]{1,0:T(8,128)S(1)}, u32[]{:S(2)}, u32[]{:S(2)}) collective-permute-start(f32[136,384]{1,0:T(8,128)S(1)} %get-tuple-element.258), channel_id=1, source_target_pairs={{0,16},{8,24},{16,0},{24,8},{1,17},{9,25},{17,1},{25,9},{2,18},{10... | collective-permute-start | bytes 626696 | tf_op jit(solution)/shard_map/ppermute | solution.py:165
  172.1 15.8 %collective-permute-start.61 = (f32[2,120,384]{2,1,0:T(8,128)S(1)}, f32[2,120,384]{2,1,0:T(8,128)S(1)}, u32[]{:S(2)}, u32[]{:S(2)}) collective-permute-start(f32[2,120,384]{2,1,0:T(8,128)S(1)} %get-tuple-element.247), channel_id=1, source_target_pairs={{0,2},{1,3},{2,0},{3,1},{4,6},{5,7},{6,4},{7,5},{8,10},{9,11},{10,... | collective-permute-start | bytes 1105928 | tf_op jit(solution)/shard_map/ppermute | solution.py:175
  173.5 8.8 %collective-permute-start.53 = (f32[136,384]{1,0:T(8,128)S(1)}, f32[136,384]{1,0:T(8,128)S(1)}, u32[]{:S(2)}, u32[]{:S(2)}) collective-permute-start(f32[136,384]{1,0:T(8,128)S(1)} %get-tuple-element.257), channel_id=1, source_target_pairs={{0,24},{8,16},{16,8},{24,0},{1,25},{9,17},{17,9},{25,1},{2,26},{10... | collective-permute-start | bytes 626696 | tf_op jit(solution)/shard_map/ppermute | solution.py:165
  187.9 17.8 %collective-permute-start.64 = (f32[2,96,384]{2,1,0:T(8,128)S(1)}, f32[2,96,384]{2,1,0:T(8,128)S(1)}, u32[]{:S(2)}, u32[]{:S(2)}) collective-permute-start(f32[2,96,384]{2,1,0:T(8,128)S(1)} %pad_maximum_fusion.9), channel_id=1, source_target_pairs={{0,2},{1,3},{2,0},{3,1},{4,6},{5,7},{6,4},{7,5},{8,10},{9,11},{10,... | collective-permute-start | bytes 884744 | tf_op jit(solution)/shard_map/ppermute | solution.py:175
  188.1 17.5 %collective-permute-start.63 = (f32[1,216,384]{2,1,0:T(8,128)S(1)}, f32[1,216,384]{2,1,0:T(8,128)S(1)}, u32[]{:S(2)}, u32[]{:S(2)}) collective-permute-start(f32[1,216,384]{2,1,0:T(8,128)S(1)} %pad_maximum_fusion.7), channel_id=1, source_target_pairs={{0,4},{1,5},{2,6},{3,7},{4,0},{5,1},{6,2},{7,3},{8,12},{9,13},{10,... | collective-permute-start | bytes 995336 | tf_op jit(solution)/shard_map/ppermute | solution.py:175
  191.2 10.4 %collective-permute-start.55 = (f32[136,384]{1,0:T(8,128)S(1)}, f32[136,384]{1,0:T(8,128)S(1)}, u32[]{:S(2)}, u32[]{:S(2)}) collective-permute-start(f32[136,384]{1,0:T(8,128)S(1)} %add_add_fusion.refs_1_), channel_id=1, source_target_pairs={{0,16},{8,24},{16,0},{24,8},{1,17},{9,25},{17,1},{25,9},{2,18},{10... | collective-permute-start | bytes 626696 | tf_op jit(solution)/shard_map/ppermute | solution.py:165
  192.4 9.2 %collective-permute-start.56 = (f32[136,384]{1,0:T(8,128)S(1)}, f32[136,384]{1,0:T(8,128)S(1)}, u32[]{:S(2)}, u32[]{:S(2)}) collective-permute-start(f32[136,384]{1,0:T(8,128)S(1)} %add_add_fusion.refs_1_), channel_id=1, source_target_pairs={{0,24},{8,16},{16,8},{24,0},{1,25},{9,17},{17,9},{25,1},{2,26},{10... | collective-permute-start | bytes 626696 | tf_op jit(solution)/shard_map/ppermute | solution.py:165
  205.8 14.9 %collective-permute-start.67 = (f32[2,96,384]{2,1,0:T(8,128)S(1)}, f32[2,96,384]{2,1,0:T(8,128)S(1)}, u32[]{:S(2)}, u32[]{:S(2)}) collective-permute-start(f32[2,96,384]{2,1,0:T(8,128)S(1)} %pad_maximum_fusion.10), channel_id=1, source_target_pairs={{0,2},{1,3},{2,0},{3,1},{4,6},{5,7},{6,4},{7,5},{8,10},{9,11},{10,... | collective-permute-start | bytes 884744 | tf_op jit(solution)/shard_map/ppermute | solution.py:175
  206.3 11.1 %collective-permute-start.66 = (f32[1,128,384]{2,1,0:T(8,128)S(1)}, f32[1,128,384]{2,1,0:T(8,128)S(1)}, u32[]{:S(2)}, u32[]{:S(2)}) collective-permute-start(f32[1,128,384]{2,1,0:T(8,128)S(1)} %pad_maximum_fusion.16), channel_id=1, source_target_pairs={{0,4},{1,5},{2,6},{3,7},{4,0},{5,1},{6,2},{7,3},{8,12},{9,13},{10,... | collective-permute-start | bytes 589832 | tf_op jit(solution)/shard_map/ppermute | solution.py:175
  208.9 8.5 %collective-permute-start.57 = (f32[128,384]{1,0:T(8,128)S(1)}, f32[128,384]{1,0:T(8,128)S(1)}, u32[]{:S(2)}, u32[]{:S(2)}) collective-permute-start(f32[128,384]{1,0:T(8,128)S(1)} %shard_map.314.refs_1_), channel_id=1, source_target_pairs={{0,8},{8,0},{16,24},{24,16},{1,9},{9,1},{17,25},{25,17},{2,10},{10... | collective-permute-start | bytes 589832 | tf_op jit(solution)/shard_map/ppermute | solution.py:165
  210.1 10.6 %collective-permute-start.58 = (f32[128,384]{1,0:T(8,128)S(1)}, f32[128,384]{1,0:T(8,128)S(1)}, u32[]{:S(2)}, u32[]{:S(2)}) collective-permute-start(f32[128,384]{1,0:T(8,128)S(1)} %shard_map.314.refs_1_), channel_id=1, source_target_pairs={{0,16},{8,24},{16,0},{24,8},{1,17},{9,25},{17,1},{25,9},{2,18},{10... | collective-permute-start | bytes 589832 | tf_op jit(solution)/shard_map/ppermute | solution.py:165
  210.9 9.7 %collective-permute-start.59 = (f32[128,384]{1,0:T(8,128)S(1)}, f32[128,384]{1,0:T(8,128)S(1)}, u32[]{:S(2)}, u32[]{:S(2)}) collective-permute-start(f32[128,384]{1,0:T(8,128)S(1)} %shard_map.314.refs_1_), channel_id=1, source_target_pairs={{0,24},{8,16},{16,8},{24,0},{1,25},{9,17},{17,9},{25,1},{2,26},{10... | collective-permute-start | bytes 589832 | tf_op jit(solution)/shard_map/ppermute | solution.py:165
  220.8 11.5 %collective-permute-start.68 = (f32[4,192,384]{2,1,0:T(8,128)S(1)}, f32[4,192,384]{2,1,0:T(8,128)S(1)}, u32[]{:S(2)}, u32[]{:S(2)}) collective-permute-start(f32[4,192,384]{2,1,0:T(8,128)S(1)} %maximum_maximum_fusion), channel_id=1, source_target_pairs={{0,1},{1,0},{2,3},{3,2},{4,5},{5,4},{6,7},{7,6},{8,9},{9,8},{10,11... | collective-permute-start | bytes 3538952 | tf_op jit(solution)/shard_map/ppermute | solution.py:170
  220.9 11.3 %collective-permute-start.69 = (f32[1,248,384]{2,1,0:T(8,128)S(1)}, f32[1,248,384]{2,1,0:T(8,128)S(1)}, u32[]{:S(2)}, u32[]{:S(2)}) collective-permute-start(f32[1,248,384]{2,1,0:T(8,128)S(1)} %pad_maximum_fusion.5), channel_id=1, source_target_pairs={{0,2},{1,3},{2,0},{3,1},{4,6},{5,7},{6,4},{7,5},{8,10},{9,11},{10,... | collective-permute-start | bytes 1142792 | tf_op jit(solution)/shard_map/ppermute | solution.py:175
  (53 other events, 369.5 us)

commit v2 on v0

--- a/solution.py
+++ b/solution.py
@@ -380,15 +380,14 @@
 
 def send_slots(core, packed, slots_own, slots_other, own, other):
     half = packed.shape[1] // 2
-    lane = lax.broadcasted_iota(jnp.int32, packed.shape, 1)
-    left = jnp.where(lane < half, packed, 0.0)
-    right = jnp.where(lane < half, 0.0, packed)
-    second = core == 1
-    top = jnp.where(second, pltpu.roll(left, half, 1), left)
-    bottom = jnp.where(second, right, pltpu.roll(right, half, 1))
-    placed = jnp.concatenate([top, bottom])
-    own[...] = select_rows(slots_own, placed)
-    other[...] = select_rows(slots_other, placed)
+    rows = jnp.concatenate([packed[:, :half], packed[:, half:]])
+    for slots, out in ((slots_own, own), (slots_other, other)):
+        sent = select_rows(slots, rows)
+        for side in range(2):
+            @pl.when(core == side)
+            def _():
+                out[:, side * half : (side + 1) * half] = sent
+                out[:, (1 - side) * half : (2 - side) * half] = jnp.zeros_like(sent)
 
 
 def conv_kernel(ids, halo, gain, conv_high, conv_low, conv_in, marks, conv_weight, conv_bias,
@@ -677,16 +676,14 @@
     second = ids[2] == 1
 
     def mine(rows):
-        return jnp.where(second, pltpu.roll(rows, half, 1), rows)
+        return jnp.where(second, rows[:, half:], rows[:, :half])
 
     total = select_rows(rows_own[...], mine(own[...])) + select_rows(
         rows_other[...], mine(other[...])
     )
     count = base.shape[0]
-    lane = lax.broadcasted_iota(jnp.int32, base.shape, 1)
-    out[...] = base[...] + jnp.where(
-        lane < half, total[:count], pltpu.roll(total[count:], half, 1)
-    )
+    out[:, :half] = base[:, :half] + total[:count]
+    out[:, half:] = base[:, half:] + total[count:]
 
 
 def whole_kernel(ids, p0, p1, p2, p3, out, held, whole, tiles):

time: 233 us -> 233 us (level)
  no operation moved by 1% of the time
where the time goes in v2:
time: 233 us; the launch traced here: 230 us
  starting transfers between devices  81.8 us (35%)
  waiting for transfers between devices  67.3 us (29%)
  Pallas kernels  64 us (27%)
  blocking collectives  12.9 us (6%)
    pallas_call x24, Pallas kernels, call(): pl.pallas_call(run, out_shape=outs, in_specs=[pl.BlockSpec(memory_space=p...  64 us
    ppermute x28, waiting for transfers between devices, chip_swap(): return lax.ppermute(value, 'wide', [(i, i ^ 2 * key) for i in range(count)])  41.8 us
    ppermute x28, starting transfers between devices, chip_swap(): return lax.ppermute(value, 'wide', [(i, i ^ 2 * key) for i in range(count)])  38.4 us
    ppermute x31, starting transfers between devices, narrow_swap(): return lax.ppermute(value, 'narrow', [(i, i ^ key) for i in range(4)])  38 us
    ppermute x31, waiting for transfers between devices, narrow_swap(): return lax.ppermute(value, 'narrow', [(i, i ^ key) for i in range(4)])  22.9 us
    all_gather x1, blocking collectives, local(): hidden_parts = lax.all_gather(hold(hidden_blocks, raw), 'narrow')  12.9 us
  transfers between devices with their start and end apart: 71, of which 31 were waited for; matrix products, arithmetic and copies ran while one was open for 1% of the time, Pallas kernels for 18%

profile of v2, /device:TPU:0, one launch (start us, length us, event | category | flops | bytes accessed | tf_op | source)
XLA Modules:
  0.0 229.7 jit_solution(14145660973241691831)
XLA Ops:
  0.7 4.6 %shard_map.297 = (f32[256,8]{1,0:T(8,128)S(1)}, bf16[160,256]{1,0:T(8,128)(2,1)S(1)}, bf16[160,256]{1,0:T(8,128)(2,1)S(1)}, bf16[256,160]{1,0:T(8,128)(2,1)S(1)}...) custom-call(s32[4]{0:T(128)S(1)} %pad_add_fusion.refs_0_, ...), custom_call_target="tpu_custom_call" | custom-call | flops 1 | bytes 1 | tf_op jit(solution)/shard_map/pallas_call | solution.py:46
  8.2 2.5 %shard_map.298 = (f32[256,768]{1,0:T(8,128)S(1)}, f32[256,768]{1,0:T(8,128)S(1)}, f32[256,384]{1,0:T(8,128)S(1)}, f32[256,384]{1,0:T(8,128)S(1)}) custom-call(s32[4]{0:T(128)S(1)} %pad_add_fusion.refs_0_, f32[256,768]{1,0:T(8,128)S(1)} %copy-done.1, f32[768]{0:T(1024)S(1)} %copy-done.6, bf16[768,384]{1,0:T(8,128)(2,1)S(1)} %get-tuple-element.130.refs_3_, ...), custom_call_target="tpu_custom_call" | custom-call | flops 1 | bytes 1 | tf_op jit(solution)/shard_map/pallas_call | solution.py:46
  12.3 2.8 %collective-permute-start.2 = (f32[80,256]{1,0:T(8,128)S(1)}, f32[80,256]{1,0:T(8,128)S(1)}, u32[]{:S(2)}, u32[]{:S(2)}) collective-permute-start(f32[80,256]{1,0:T(8,128)S(1)} %get-tuple-element.138.refs_1_), channel_id=1, source_target_pairs={{0,8},{8,0},{16,24},{24,16},{1,9},{9,1},{17,25},{25,17},{2,10},{10... | collective-permute-start | bytes 245768 | tf_op jit(solution)/shard_map/ppermute | solution.py:165
  18.8 2.6 %collective-permute-start.7 = (f32[40,384]{1,0:T(8,128)S(1)}, f32[40,384]{1,0:T(8,128)S(1)}, u32[]{:S(2)}, u32[]{:S(2)}) collective-permute-start(f32[40,384]{1,0:T(8,128)S(1)} %get-tuple-element.281), channel_id=1, source_target_pairs={{0,4},{1,5},{2,6},{3,7},{4,0},{5,1},{6,2},{7,3},{8,12},{9,13},{10,... | collective-permute-start | bytes 184328 | tf_op jit(solution)/shard_map/ppermute | solution.py:175
  22.6 2.6 %shard_map.300 = (f32[256,128]{1,0:T(8,128)S(1)}, f32[256,384]{1,0:T(8,128)S(1)}, f32[256,384]{1,0:T(8,128)S(1)}, f32[256,384]{1,0:T(8,128)S(1)}, f32[256,384]{1...) custom-call(s32[4]{0:T(128)S(1)} %pad_add_fusion.refs_0_, ...), custom_call_target="tpu_custom_call" | custom-call | flops 1 | bytes 1 | tf_op jit(solution)/shard_map/pallas_call | solution.py:46
  34.7 2.2 collective-permute-done.10.refs_13_.refs_20_
  38.7 4.4 %shard_map.302 = (f32[256,384]{1,0:T(8,128)S(1)}, f32[256,384]{1,0:T(8,128)S(1)}, f32[4,128,384]{2,1,0:T(8,128)S(1)}, f32[4,33,4,8,384]{4,3,2,1,0:T(8,128)S(1)}) custom-call(s32[4]{0:T(128)S(1)} %pad_add_fusion.refs_0_, f32[256,384]{1,0:T(8,128)S(1)} %get-tuple-element.140.refs_1_.refs_9_, f32[256,384]{1,0:T(8,128)S(1)} %get-tuple-element.141.refs_2_, ...), custom_call_target="tpu_custom_call" | custom-call | flops 1 | bytes 1 | tf_op jit(solution)/shard_map/pallas_call | solution.py:46
  44.4 2.4 %collective-permute-start.16 = (f32[128,384]{1,0:T(8,128)S(1)}, f32[128,384]{1,0:T(8,128)S(1)}, u32[]{:S(2)}, u32[]{:S(2)}) collective-permute-start(f32[128,384]{1,0:T(8,128)S(1)} %get-tuple-element.261), channel_id=1, source_target_pairs={{0,24},{8,16},{16,8},{24,0},{1,25},{9,17},{17,9},{25,1},{2,26},{10... | collective-permute-start | bytes 589832 | tf_op jit(solution)/shard_map/ppermute | solution.py:165
  46.8 3.3 %collective-permute-done.14.refs_2_ = f32[128,384]{1,0:T(8,128)S(1)} collective-permute-done((f32[128,384]{1,0:T(8,128)S(1)}, f32[128,384]{1,0:T(8,128)S(1)}, u32[]{:S(2)}, u32[]{:S(2)}) %collective-permute-start.14) | collective-permute-done | bytes 196640 | tf_op jit(solution)/shard_map/ppermute | solution.py:165
  50.1 2.4 %collective-permute-done.15.refs_3_ = f32[128,384]{1,0:T(8,128)S(1)} collective-permute-done((f32[128,384]{1,0:T(8,128)S(1)}, f32[128,384]{1,0:T(8,128)S(1)}, u32[]{:S(2)}, u32[]{:S(2)}) %collective-permute-start.15) | collective-permute-done | bytes 196640 | tf_op jit(solution)/shard_map/ppermute | solution.py:165
  56.2 2.3 collective-permute-start.19
  60.6 2.8 %shard_map.304 = (f32[320,768]{1,0:T(8,128)S(1)}, f32[320,768]{1,0:T(8,128)S(1)}, bf16[768,768]{1,0:T(8,128)(2,1)S(1)}, bf16[768,768]{1,0:T(8,128)(2,1)S(1)}, bf...) custom-call(s32[4]{0:T(128)S(1)} %pad_add_fusion.refs_0_, f32[160,384]{1,0:T(8,128)S(1)} %pad_maximum_fusion.11.refs_4_.refs_1_, ...), custom_call_target="tpu_custom_call" | custom-call | flops 1 | bytes 1 | tf_op jit(solution)/shard_map/pallas_call | solution.py:46
  64.7 12.9 %all-gather = f32[640,384]{1,0:T(8,128)S(1)} all-gather(f32[160,384]{1,0:T(8,128)S(1)} %pad_maximum_fusion.12), channel_id=2, replica_groups=mesh['narrow'=4,'wide'=8] {'narrow'}, dimensions={0}, use_global_device_ids=true | all-gather | bytes 1228800 | tf_op jit(solution)/shard_map/all_gather | solution.py:1130
  77.5 5.8 %shard_map.305 = (f32[4,160,384]{2,1,0:T(8,128)S(1)}, f32[320,768]{1,0:T(8,128)S(1)}, f32[320,768]{1,0:T(8,128)S(1)}, f32[320,768]{1,0:T(8,128)S(1)}, f32[320,1]...) custom-call(s32[4]{0:T(128)S(1)} %pad_add_fusion.refs_0_, f32[4,160,384]{2,1,0:T(8,128)S(1)} %bitcast.58, ...), custom_call_target="tpu_custom_call" | custom-call | flops 1 | bytes 1 | tf_op jit(solution)/shard_map/pallas_call | solution.py:46
  87.0 7.3 %shard_map.306 = (f32[4,160,384]{2,1,0:T(8,128)S(1)}, f32[768,768]{1,0:T(8,128)}, f32[768,768]{1,0:T(8,128)}, f32[8,768]{1,0:T(8,128)S(1)}) custom-call(s32[4]{0:T(128)S(1)} %pad_add_fusion.refs_0_, f32[320,768]{1,0:T(8,128)S(1)} %get-tuple-element.164.refs_1_, f32[320,768]{1,0:T(8,128)S(1)} %get-tuple-element.165.refs_2_, ...), custom_call_target="tpu_custom_call" | custom-call | flops 1 | bytes 1 | tf_op jit(solution)/shard_map/pallas_call | solution.py:46
  98.7 2.2 collective-permute-start.33
  104.5 2.6 %collective-permute-done.34 = f32[40,384]{1,0:T(8,128)S(1)} collective-permute-done((f32[40,384]{1,0:T(8,128)S(1)}, f32[40,384]{1,0:T(8,128)S(1)}, u32[]{:S(2)}, u32[]{:S(2)}) %collective-permute-start.34) | collective-permute-done | bytes 61472 | tf_op jit(solution)/shard_map/ppermute | solution.py:175
  116.4 4.2 %collective-permute-done.27 = f32[40,384]{1,0:T(8,128)S(1)} collective-permute-done((f32[40,384]{1,0:T(8,128)S(1)}, f32[40,384]{1,0:T(8,128)S(1)}, u32[]{:S(2)}, u32[]{:S(2)}) %collective-permute-start.27) | collective-permute-done | bytes 61472 | tf_op jit(solution)/shard_map/ppermute | solution.py:175
  121.8 3.3 %shard_map.308 = (f32[256,768]{1,0:T(8,128)S(1)}, f32[256,384]{1,0:T(8,128)S(1)}, f32[256,384]{1,0:T(8,128)S(1)}, f32[1,384]{1,0:T(1,128)S(1)}, f32[2,16,8,384]{3,2,1,0:T(8,128)S(1)}, /*index=5*/f32[16,384]{1,0:T(8,128)S(1)}) custom-call(s32[4]{0:T(128)S(1)} %pad_add_fusion.refs_0_, f32[128,384]{1,0:T(8,128)S(1)} %shard_map.307.refs_1_, ...), custom_call_target="tpu_custom_call" | custom-call | flops 1 | bytes 1 | tf_op jit(solution)/shard_map/pallas_call | solution.py:46
  133.8 2.7 %collective-permute-done.42.refs_25_ = f32[16,384]{1,0:T(8,128)S(1)} collective-permute-done((f32[16,384]{1,0:T(8,128)S(1)}, f32[16,384]{1,0:T(8,128)S(1)}, u32[]{:S(2)}, u32[]{:S(2)}) %collective-permute-start.42) | collective-permute-done | bytes 24608 | tf_op jit(solution)/shard_map/ppermute | solution.py:175
  136.5 7.1 %shard_map.311 = (f32[112,256]{1,0:T(8,128)S(1)}, f32[256,384]{1,0:T(8,128)S(1)}, f32[256,384]{1,0:T(8,128)S(1)}, f32[16,384]{1,0:T(8,128)S(1)}, f32[1,384]{1,0:T(1,128)S(1)}) custom-call(s32[4]{0:T(128)S(1)} %pad_add_fusion.refs_0_, f32[256,384]{1,0:T(8,128)S(1)} %get-tuple-element.140.refs_1_.refs_9_, f32[256,384]{1,0:T(8,128)S(1)} %get-tuple-element.141.refs_2_, ...), custom_call_target="tpu_custom_call" | custom-call | flops 1 | bytes 1 | tf_op jit(solution)/shard_map/pallas_call | solution.py:46
  154.1 2.7 %shard_map.312 = (f32[4,120,384]{2,1,0:T(8,128)S(1)}, f32[4,120,384]{2,1,0:T(8,128)S(1)}, f32[256,384]{1,0:T(8,128)S(1)}, f32[8,384]{1,0:T(8,128)S(1)}) custom-call(s32[4]{0:T(128)S(1)} %pad_add_fusion.refs_0_, f32[112,256]{1,0:T(8,128)S(1)} %get-tuple-element.196.refs_1_.refs_4_, f32[112,256]{1,0:T(8,128)S(1)} %collective-permute-done.44.refs_2_, ...), custom_call_target="tpu_custom_call" | custom-call | flops 1 | bytes 1 | tf_op jit(solution)/shard_map/pallas_call | solution.py:46
  157.1 2.7 %collective-permute-start.62 = (f32[1,192,384]{2,1,0:T(8,128)S(1)}, f32[1,192,384]{2,1,0:T(8,128)S(1)}, u32[]{:S(2)}, u32[]{:S(2)}) collective-permute-start(f32[1,192,384]{2,1,0:T(8,128)S(1)} %pad_maximum_fusion.8), channel_id=1, source_target_pairs={{0,4},{1,5},{2,6},{3,7},{4,0},{5,1},{6,2},{7,3},{8,12},{9,13},{10,... | collective-permute-start | bytes 884744 | tf_op jit(solution)/shard_map/ppermute | solution.py:175
  168.0 5.9 %collective-permute-done.62 = f32[1,192,384]{2,1,0:T(8,128)S(1)} collective-permute-done((f32[1,192,384]{2,1,0:T(8,128)S(1)}, f32[1,192,384]{2,1,0:T(8,128)S(1)}, u32[]{:S(2)}, u32[]{:S(2)}) %collective-permute-start.62) | collective-permute-done | bytes 294944 | tf_op jit(solution)/shard_map/ppermute | solution.py:175
  174.1 5.7 %collective-permute-done.61 = f32[2,120,384]{2,1,0:T(8,128)S(1)} collective-permute-done((f32[2,120,384]{2,1,0:T(8,128)S(1)}, f32[2,120,384]{2,1,0:T(8,128)S(1)}, u32[]{:S(2)}, u32[]{:S(2)}) %collective-permute-start.61) | collective-permute-done | bytes 368672 | tf_op jit(solution)/shard_map/ppermute | solution.py:175
  185.7 4.6 %collective-permute-done.54.refs_2_ = f32[136,384]{1,0:T(8,128)S(1)} collective-permute-done((f32[136,384]{1,0:T(8,128)S(1)}, f32[136,384]{1,0:T(8,128)S(1)}, u32[]{:S(2)}, u32[]{:S(2)}) %collective-permute-start.54) | collective-permute-done | bytes 208928 | tf_op jit(solution)/shard_map/ppermute | solution.py:165
  190.3 3.6 %collective-permute-done.55.refs_3_ = f32[136,384]{1,0:T(8,128)S(1)} collective-permute-done((f32[136,384]{1,0:T(8,128)S(1)}, f32[136,384]{1,0:T(8,128)S(1)}, u32[]{:S(2)}, u32[]{:S(2)}) %collective-permute-start.55) | collective-permute-done | bytes 208928 | tf_op jit(solution)/shard_map/ppermute | solution.py:165
  204.0 2.7 %shard_map.318 = f32[256,768]{1,0:T(8,128)} custom-call(s32[4]{0:T(128)S(1)} %pad_add_fusion.refs_0_, f32[136,384]{1,0:T(8,128)S(1)} %add_add_fusion.refs_1_, f32[136,384]{1,0:T(8,128)S(1)} %collective-permute-done.54.refs_2_, f32[136,384]{1,0:T(8,128)S(1)} %collective-permute-done.55.refs_3_, f32[136,384]{1,0:T(8,128)S(1)} %collective-permute-done.56.refs_4_, ...), custom_call_target="tpu_custom_call" | custom-call | flops 1 | bytes 1 | tf_op jit(solution)/shard_map/pallas_call | solution.py:46
  206.8 3.3 %collective-permute-done.66 = f32[1,128,384]{2,1,0:T(8,128)S(1)} collective-permute-done((f32[1,128,384]{2,1,0:T(8,128)S(1)}, f32[1,128,384]{2,1,0:T(8,128)S(1)}, u32[]{:S(2)}, u32[]{:S(2)}) %collective-permute-start.66) | collective-permute-done | bytes 196640 | tf_op jit(solution)/shard_map/ppermute | solution.py:175
  210.1 2.5 %collective-permute-done.58.refs_3_ = f32[128,384]{1,0:T(8,128)S(1)} collective-permute-done((f32[128,384]{1,0:T(8,128)S(1)}, f32[128,384]{1,0:T(8,128)S(1)}, u32[]{:S(2)}, u32[]{:S(2)}) %collective-permute-start.58) | collective-permute-done | bytes 196640 | tf_op jit(solution)/shard_map/ppermute | solution.py:165
  216.9 7.3 %collective-permute-done.69 = f32[1,248,384]{2,1,0:T(8,128)S(1)} collective-permute-done((f32[1,248,384]{2,1,0:T(8,128)S(1)}, f32[1,248,384]{2,1,0:T(8,128)S(1)}, u32[]{:S(2)}, u32[]{:S(2)}) %collective-permute-start.69) | collective-permute-done | bytes 380960 | tf_op jit(solution)/shard_map/ppermute | solution.py:175
  226.9 2.5 %shard_map.320 = (f32[768,2,384]{2,1,0:T(2,128)}, f32[80,384]{1,0:T(8,128)}, f32[48,384]{1,0:T(8,128)}, f32[16,384]{1,0:T(8,128)}, f32[4,384]{1,0:T(4,128)}, /*i...) custom-call(s32[4]{0:T(128)S(1)} %pad_add_fusion.refs_0_, ...), custom_call_target="tpu_custom_call" | custom-call | flops 1 | bytes 1 | tf_op jit(solution)/shard_map/pallas_call | solution.py:46
  (216 shorter events, 101.6 us)
Async XLA Ops:
  12.3 9.1 %collective-permute-start.2 = (f32[80,256]{1,0:T(8,128)S(1)}, f32[80,256]{1,0:T(8,128)S(1)}, u32[]{:S(2)}, u32[]{:S(2)}) collective-permute-start(f32[80,256]{1,0:T(8,128)S(1)} %get-tuple-element.138.refs_1_), channel_id=1, source_target_pairs={{0,8},{8,0},{16,24},{24,16},{1,9},{9,1},{17,25},{25,17},{2,10},{10... | collective-permute-start | bytes 245768 | tf_op jit(solution)/shard_map/ppermute | solution.py:165
  16.7 8.6 %collective-permute-start.6 = (f32[40,384]{1,0:T(8,128)S(1)}, f32[40,384]{1,0:T(8,128)S(1)}, u32[]{:S(2)}, u32[]{:S(2)}) collective-permute-start(f32[40,384]{1,0:T(8,128)S(1)} %get-tuple-element.282), channel_id=1, source_target_pairs={{0,2},{1,3},{2,0},{3,1},{4,6},{5,7},{6,4},{7,5},{8,10},{9,11},{10,... | collective-permute-start | bytes 184328 | tf_op jit(solution)/shard_map/ppermute | solution.py:175
  28.1 15.0 %collective-permute-start.12 = (f32[160,384]{1,0:T(8,128)S(1)}, f32[160,384]{1,0:T(8,128)S(1)}, u32[]{:S(2)}, u32[]{:S(2)}) collective-permute-start(f32[160,384]{1,0:T(8,128)S(1)} %pad_maximum_fusion.11.refs_4_.refs_1_), channel_id=1, source_target_pairs={{0,8},{8,0},{16,24},{24,16},{1,9},{9,1},{17,25},{25,17},{2,10},{10... | collective-permute-start | bytes 737288 | tf_op jit(solution)/shard_map/ppermute | solution.py:165
  29.7 13.5 %collective-permute-start.13 = (f32[160,384]{1,0:T(8,128)S(1)}, f32[160,384]{1,0:T(8,128)S(1)}, u32[]{:S(2)}, u32[]{:S(2)}) collective-permute-start(f32[160,384]{1,0:T(8,128)S(1)} %pad_maximum_fusion.11.refs_4_.refs_1_), channel_id=1, source_target_pairs={{0,16},{8,24},{16,0},{24,8},{1,17},{9,25},{17,1},{25,9},{2,18},{10... | collective-permute-start | bytes 737288 | tf_op jit(solution)/shard_map/ppermute | solution.py:165
  43.9 8.7 %collective-permute-start.15 = (f32[128,384]{1,0:T(8,128)S(1)}, f32[128,384]{1,0:T(8,128)S(1)}, u32[]{:S(2)}, u32[]{:S(2)}) collective-permute-start(f32[128,384]{1,0:T(8,128)S(1)} %get-tuple-element.262), channel_id=1, source_target_pairs={{0,16},{8,24},{16,0},{24,8},{1,17},{9,25},{17,1},{25,9},{2,18},{10... | collective-permute-start | bytes 589832 | tf_op jit(solution)/shard_map/ppermute | solution.py:165
  56.2 8.5 %collective-permute-start.19 = (f32[40,384]{1,0:T(8,128)S(1)}, f32[40,384]{1,0:T(8,128)S(1)}, u32[]{:S(2)}, u32[]{:S(2)}) collective-permute-start(f32[40,384]{1,0:T(8,128)S(1)} %get-tuple-element.277), channel_id=1, source_target_pairs={{0,4},{1,5},{2,6},{3,7},{4,0},{5,1},{6,2},{7,3},{8,12},{9,13},{10,... | collective-permute-start | bytes 184328 | tf_op jit(solution)/shard_map/ppermute | solution.py:175
  83.4 13.0 %collective-permute-start.29 = (f32[160,384]{1,0:T(8,128)S(1)}, f32[160,384]{1,0:T(8,128)S(1)}, u32[]{:S(2)}, u32[]{:S(2)}) collective-permute-start(f32[160,384]{1,0:T(8,128)S(1)} %get-tuple-element.254), channel_id=1, source_target_pairs={{0,8},{8,0},{16,24},{24,16},{1,9},{9,1},{17,25},{25,17},{2,10},{10... | collective-permute-start | bytes 737288 | tf_op jit(solution)/shard_map/ppermute | solution.py:165
  83.8 14.1 %collective-permute-start.30 = (f32[160,384]{1,0:T(8,128)S(1)}, f32[160,384]{1,0:T(8,128)S(1)}, u32[]{:S(2)}, u32[]{:S(2)}) collective-permute-start(f32[160,384]{1,0:T(8,128)S(1)} %get-tuple-element.253), channel_id=1, source_target_pairs={{0,16},{8,24},{16,0},{24,8},{1,17},{9,25},{17,1},{25,9},{2,18},{10... | collective-permute-start | bytes 737288 | tf_op jit(solution)/shard_map/ppermute | solution.py:165
  85.5 12.4 %collective-permute-start.31 = (f32[160,384]{1,0:T(8,128)S(1)}, f32[160,384]{1,0:T(8,128)S(1)}, u32[]{:S(2)}, u32[]{:S(2)}) collective-permute-start(f32[160,384]{1,0:T(8,128)S(1)} %get-tuple-element.252), channel_id=1, source_target_pairs={{0,24},{8,16},{16,8},{24,0},{1,25},{9,17},{17,9},{25,1},{2,26},{10... | collective-permute-start | bytes 737288 | tf_op jit(solution)/shard_map/ppermute | solution.py:165
  94.7 9.7 %collective-permute-start.24 = (f32[160,384]{1,0:T(8,128)S(1)}, f32[160,384]{1,0:T(8,128)S(1)}, u32[]{:S(2)}, u32[]{:S(2)}) collective-permute-start(f32[160,384]{1,0:T(8,128)S(1)} %get-tuple-element.256), channel_id=1, source_target_pairs={{0,16},{8,24},{16,0},{24,8},{1,17},{9,25},{17,1},{25,9},{2,18},{10... | collective-permute-start | bytes 737288 | tf_op jit(solution)/shard_map/ppermute | solution.py:165
  109.7 11.0 %collective-permute-start.36 = (f32[128,384]{1,0:T(8,128)S(1)}, f32[128,384]{1,0:T(8,128)S(1)}, u32[]{:S(2)}, u32[]{:S(2)}) collective-permute-start(f32[128,384]{1,0:T(8,128)S(1)} %shard_map.307.refs_1_), channel_id=1, source_target_pairs={{0,8},{8,0},{16,24},{24,16},{1,9},{9,1},{17,25},{25,17},{2,10},{10... | collective-permute-start | bytes 589832 | tf_op jit(solution)/shard_map/ppermute | solution.py:165
  110.9 10.9 %collective-permute-start.37 = (f32[128,384]{1,0:T(8,128)S(1)}, f32[128,384]{1,0:T(8,128)S(1)}, u32[]{:S(2)}, u32[]{:S(2)}) collective-permute-start(f32[128,384]{1,0:T(8,128)S(1)} %shard_map.307.refs_1_), channel_id=1, source_target_pairs={{0,16},{8,24},{16,0},{24,8},{1,17},{9,25},{17,1},{25,9},{2,18},{10... | collective-permute-start | bytes 589832 | tf_op jit(solution)/shard_map/ppermute | solution.py:165
  111.8 10.0 %collective-permute-start.38 = (f32[128,384]{1,0:T(8,128)S(1)}, f32[128,384]{1,0:T(8,128)S(1)}, u32[]{:S(2)}, u32[]{:S(2)}) collective-permute-start(f32[128,384]{1,0:T(8,128)S(1)} %shard_map.307.refs_1_), channel_id=1, source_target_pairs={{0,24},{8,16},{16,8},{24,0},{1,25},{9,17},{17,9},{25,1},{2,26},{10... | collective-permute-start | bytes 589832 | tf_op jit(solution)/shard_map/ppermute | solution.py:165
  136.5 9.2 %collective-permute-start.48 = (f32[2,96,384]{2,1,0:T(8,128)S(1)}, f32[2,96,384]{2,1,0:T(8,128)S(1)}, u32[]{:S(2)}, u32[]{:S(2)}) collective-permute-start(f32[2,96,384]{2,1,0:T(8,128)S(1)} %get-tuple-element.206.refs_26_), channel_id=1, source_target_pairs={{0,2},{1,3},{2,0},{3,1},{4,6},{5,7},{6,4},{7,5},{8,10},{9,11},{10,... | collective-permute-start | bytes 884744 | tf_op jit(solution)/shard_map/ppermute | solution.py:175
  143.6 10.6 %collective-permute-start.47 = (f32[2,96,384]{2,1,0:T(8,128)S(1)}, f32[2,96,384]{2,1,0:T(8,128)S(1)}, u32[]{:S(2)}, u32[]{:S(2)}) collective-permute-start(f32[2,96,384]{2,1,0:T(8,128)S(1)} %get-tuple-element.205.refs_27_), channel_id=1, source_target_pairs={{0,2},{1,3},{2,0},{3,1},{4,6},{5,7},{6,4},{7,5},{8,10},{9,11},{10,... | collective-permute-start | bytes 884744 | tf_op jit(solution)/shard_map/ppermute | solution.py:175
  145.7 8.5 %collective-permute-start.49 = (f32[1,96,384]{2,1,0:T(8,128)S(1)}, f32[1,96,384]{2,1,0:T(8,128)S(1)}, u32[]{:S(2)}, u32[]{:S(2)}) collective-permute-start(f32[1,96,384]{2,1,0:T(8,128)S(1)} %slice_add_fusion.11), channel_id=1, source_target_pairs={{0,4},{1,5},{2,6},{3,7},{4,0},{5,1},{6,2},{7,3},{8,12},{9,13},{10,... | collective-permute-start | bytes 442376 | tf_op jit(solution)/shard_map/ppermute | solution.py:175
  157.1 16.8 %collective-permute-start.62 = (f32[1,192,384]{2,1,0:T(8,128)S(1)}, f32[1,192,384]{2,1,0:T(8,128)S(1)}, u32[]{:S(2)}, u32[]{:S(2)}) collective-permute-start(f32[1,192,384]{2,1,0:T(8,128)S(1)} %pad_maximum_fusion.8), channel_id=1, source_target_pairs={{0,4},{1,5},{2,6},{3,7},{4,0},{5,1},{6,2},{7,3},{8,12},{9,13},{10,... | collective-permute-start | bytes 884744 | tf_op jit(solution)/shard_map/ppermute | solution.py:175
  161.8 12.1 %collective-permute-start.51 = (f32[136,384]{1,0:T(8,128)S(1)}, f32[136,384]{1,0:T(8,128)S(1)}, u32[]{:S(2)}, u32[]{:S(2)}) collective-permute-start(f32[136,384]{1,0:T(8,128)S(1)} %get-tuple-element.258), channel_id=1, source_target_pairs={{0,8},{8,0},{16,24},{24,16},{1,9},{9,1},{17,25},{25,17},{2,10},{10... | collective-permute-start | bytes 626696 | tf_op jit(solution)/shard_map/ppermute | solution.py:165
  162.6 11.5 %collective-permute-start.52 = (f32[136,384]{1,0:T(8,128)S(1)}, f32[136,384]{1,0:T(8,128)S(1)}, u32[]{:S(2)}, u32[]{:S(2)}) collective-permute-start(f32[136,384]{1,0:T(8,128)S(1)} %get-tuple-element.260), channel_id=1, source_target_pairs={{0,16},{8,24},{16,0},{24,8},{1,17},{9,25},{17,1},{25,9},{2,18},{10... | collective-permute-start | bytes 626696 | tf_op jit(solution)/shard_map/ppermute | solution.py:165
  164.0 15.8 %collective-permute-start.61 = (f32[2,120,384]{2,1,0:T(8,128)S(1)}, f32[2,120,384]{2,1,0:T(8,128)S(1)}, u32[]{:S(2)}, u32[]{:S(2)}) collective-permute-start(f32[2,120,384]{2,1,0:T(8,128)S(1)} %get-tuple-element.249), channel_id=1, source_target_pairs={{0,2},{1,3},{2,0},{3,1},{4,6},{5,7},{6,4},{7,5},{8,10},{9,11},{10,... | collective-permute-start | bytes 1105928 | tf_op jit(solution)/shard_map/ppermute | solution.py:175
  165.4 8.7 %collective-permute-start.53 = (f32[136,384]{1,0:T(8,128)S(1)}, f32[136,384]{1,0:T(8,128)S(1)}, u32[]{:S(2)}, u32[]{:S(2)}) collective-permute-start(f32[136,384]{1,0:T(8,128)S(1)} %get-tuple-element.259), channel_id=1, source_target_pairs={{0,24},{8,16},{16,8},{24,0},{1,25},{9,17},{17,9},{25,1},{2,26},{10... | collective-permute-start | bytes 626696 | tf_op jit(solution)/shard_map/ppermute | solution.py:165
  179.8 18.0 %collective-permute-start.64 = (f32[2,96,384]{2,1,0:T(8,128)S(1)}, f32[2,96,384]{2,1,0:T(8,128)S(1)}, u32[]{:S(2)}, u32[]{:S(2)}) collective-permute-start(f32[2,96,384]{2,1,0:T(8,128)S(1)} %pad_maximum_fusion.9), channel_id=1, source_target_pairs={{0,2},{1,3},{2,0},{3,1},{4,6},{5,7},{6,4},{7,5},{8,10},{9,11},{10,... | collective-permute-start | bytes 884744 | tf_op jit(solution)/shard_map/ppermute | solution.py:175
  180.0 17.5 %collective-permute-start.63 = (f32[1,216,384]{2,1,0:T(8,128)S(1)}, f32[1,216,384]{2,1,0:T(8,128)S(1)}, u32[]{:S(2)}, u32[]{:S(2)}) collective-permute-start(f32[1,216,384]{2,1,0:T(8,128)S(1)} %pad_maximum_fusion.7), channel_id=1, source_target_pairs={{0,4},{1,5},{2,6},{3,7},{4,0},{5,1},{6,2},{7,3},{8,12},{9,13},{10,... | collective-permute-start | bytes 995336 | tf_op jit(solution)/shard_map/ppermute | solution.py:175
  183.4 10.4 %collective-permute-start.55 = (f32[136,384]{1,0:T(8,128)S(1)}, f32[136,384]{1,0:T(8,128)S(1)}, u32[]{:S(2)}, u32[]{:S(2)}) collective-permute-start(f32[136,384]{1,0:T(8,128)S(1)} %add_add_fusion.refs_1_), channel_id=1, source_target_pairs={{0,16},{8,24},{16,0},{24,8},{1,17},{9,25},{17,1},{25,9},{2,18},{10... | collective-permute-start | bytes 626696 | tf_op jit(solution)/shard_map/ppermute | solution.py:165
  184.2 9.6 %collective-permute-start.56 = (f32[136,384]{1,0:T(8,128)S(1)}, f32[136,384]{1,0:T(8,128)S(1)}, u32[]{:S(2)}, u32[]{:S(2)}) collective-permute-start(f32[136,384]{1,0:T(8,128)S(1)} %add_add_fusion.refs_1_), channel_id=1, source_target_pairs={{0,24},{8,16},{16,8},{24,0},{1,25},{9,17},{17,9},{25,1},{2,26},{10... | collective-permute-start | bytes 626696 | tf_op jit(solution)/shard_map/ppermute | solution.py:165
  197.8 14.8 %collective-permute-start.67 = (f32[2,96,384]{2,1,0:T(8,128)S(1)}, f32[2,96,384]{2,1,0:T(8,128)S(1)}, u32[]{:S(2)}, u32[]{:S(2)}) collective-permute-start(f32[2,96,384]{2,1,0:T(8,128)S(1)} %pad_maximum_fusion.10), channel_id=1, source_target_pairs={{0,2},{1,3},{2,0},{3,1},{4,6},{5,7},{6,4},{7,5},{8,10},{9,11},{10,... | collective-permute-start | bytes 884744 | tf_op jit(solution)/shard_map/ppermute | solution.py:175
  198.6 11.5 %collective-permute-start.66 = (f32[1,128,384]{2,1,0:T(8,128)S(1)}, f32[1,128,384]{2,1,0:T(8,128)S(1)}, u32[]{:S(2)}, u32[]{:S(2)}) collective-permute-start(f32[1,128,384]{2,1,0:T(8,128)S(1)} %pad_maximum_fusion.16), channel_id=1, source_target_pairs={{0,4},{1,5},{2,6},{3,7},{4,0},{5,1},{6,2},{7,3},{8,12},{9,13},{10,... | collective-permute-start | bytes 589832 | tf_op jit(solution)/shard_map/ppermute | solution.py:175
  200.6 9.5 %collective-permute-start.57 = (f32[128,384]{1,0:T(8,128)S(1)}, f32[128,384]{1,0:T(8,128)S(1)}, u32[]{:S(2)}, u32[]{:S(2)}) collective-permute-start(f32[128,384]{1,0:T(8,128)S(1)} %shard_map.313.refs_1_), channel_id=1, source_target_pairs={{0,8},{8,0},{16,24},{24,16},{1,9},{9,1},{17,25},{25,17},{2,10},{10... | collective-permute-start | bytes 589832 | tf_op jit(solution)/shard_map/ppermute | solution.py:165
  202.0 10.6 %collective-permute-start.58 = (f32[128,384]{1,0:T(8,128)S(1)}, f32[128,384]{1,0:T(8,128)S(1)}, u32[]{:S(2)}, u32[]{:S(2)}) collective-permute-start(f32[128,384]{1,0:T(8,128)S(1)} %shard_map.313.refs_1_), channel_id=1, source_target_pairs={{0,16},{8,24},{16,0},{24,8},{1,17},{9,25},{17,1},{25,9},{2,18},{10... | collective-permute-start | bytes 589832 | tf_op jit(solution)/shard_map/ppermute | solution.py:165
  202.6 10.0 %collective-permute-start.59 = (f32[128,384]{1,0:T(8,128)S(1)}, f32[128,384]{1,0:T(8,128)S(1)}, u32[]{:S(2)}, u32[]{:S(2)}) collective-permute-start(f32[128,384]{1,0:T(8,128)S(1)} %shard_map.313.refs_1_), channel_id=1, source_target_pairs={{0,24},{8,16},{16,8},{24,0},{1,25},{9,17},{17,9},{25,1},{2,26},{10... | collective-permute-start | bytes 589832 | tf_op jit(solution)/shard_map/ppermute | solution.py:165
  212.7 11.5 %collective-permute-start.68 = (f32[4,192,384]{2,1,0:T(8,128)S(1)}, f32[4,192,384]{2,1,0:T(8,128)S(1)}, u32[]{:S(2)}, u32[]{:S(2)}) collective-permute-start(f32[4,192,384]{2,1,0:T(8,128)S(1)} %maximum_maximum_fusion), channel_id=1, source_target_pairs={{0,1},{1,0},{2,3},{3,2},{4,5},{5,4},{6,7},{7,6},{8,9},{9,8},{10,11... | collective-permute-start | bytes 3538952 | tf_op jit(solution)/shard_map/ppermute | solution.py:170
  212.9 11.3 %collective-permute-start.69 = (f32[1,248,384]{2,1,0:T(8,128)S(1)}, f32[1,248,384]{2,1,0:T(8,128)S(1)}, u32[]{:S(2)}, u32[]{:S(2)}) collective-permute-start(f32[1,248,384]{2,1,0:T(8,128)S(1)} %pad_maximum_fusion.5), channel_id=1, source_target_pairs={{0,2},{1,3},{2,0},{3,1},{4,6},{5,7},{6,4},{7,5},{8,10},{9,11},{10,... | collective-permute-start | bytes 1142792 | tf_op jit(solution)/shard_map/ppermute | solution.py:175
  (53 other events, 375.2 us)
